TPU v7x, 512 devices: a whole 4x8x8 slice. The times are simulated.
512 devices in a mesh: aux: 64 (over y, x, z_lo), basis: 8 (over z_hi, core).
Axes of the slice: x: 4, y: 8, z: 8 (z_hi: 4, z_lo: 2; z = z_hi * 2 + z_lo), core: 2. Of those that a mesh axis runs over, the one named last changes fastest.
Arguments:
- integrals: float32 [128, 512, 4096], P('aux', None, 'basis'), may hold values from -0.75 to 0.75
- occupied: float32 [4096, 768], P('basis', 'aux'), may hold values from -0.09375 to 0.09375
Outputs:
- exchange: float32 [256, 256], P('aux', 'basis')
All inputs are finite; a program needn't handle non-finite values.
Results may differ from a plain program's by a relative error of at most 0.000078.
Values sent between devices are 32-bit elements; how exact they have to be, the bound alone decides.
No kernel may reach another device: no remote copies, remote signals or barrier semaphores. Data moves between devices by JAX's collectives and lax.ppermute only.
A program may use at most 64 MiB of HBM per device.

v0:
```python
import jax
import jax.numpy as jnp
from jax import lax
from jax.sharding import PartitionSpec as P


def body(integrals, occupied):
    row_count = integrals.shape[1] // 2
    share_width = row_count // lax.axis_size("basis")
    partial_x = jnp.einsum(
        "prl,li->pri",
        integrals,
        lax.all_gather(occupied, "aux", axis=1, tiled=True),
        precision=lax.Precision.HIGHEST,
    )
    summed = lax.psum(partial_x, "basis")
    offset = lax.axis_index("basis") * share_width
    column_block = lax.dynamic_slice_in_dim(summed, row_count + offset, share_width, 1)
    tile_part = jnp.einsum(
        "pmi,pni->mn", summed[:, :row_count], column_block, precision=lax.Precision.HIGHEST
    )
    return lax.psum_scatter(tile_part, "aux", scatter_dimension=0, tiled=True)


def solution(mesh):
    placed = (P("aux", None, "basis"), P("basis", "aux"))
    return jax.shard_map(
        body, mesh=mesh, in_specs=placed, out_specs=P("aux", "basis"), check_vma=False
    )
```

profile of v0, /device:TPU:32, one launch (start us, length us, event | category | flops | bytes accessed | tf_op | source)
XLA Modules:
  0.0 744.9 jit_solution(6654432845411720987)
XLA Ops:
  6.5 0.0 copy-start
  6.5 0.0 all-gather.3.cloned.1.call-start
  6.5 0.7 all-gather.3.cloned.1.call-update
  7.3 0.0 all-reduce.3.cloned.1.call-start
  7.3 306.3 %all-gather.3.cloned.1.call-done = f32[64,12,512]{2,1,0:T(8,128)} async-done(((f32[1,12,512]{2,1,0:T(8,128)}), f32[64,12,512]{2,1,0:T(8,128)}) %all-gather.3.cloned.1.call-update) | async-done | bytes 1572880 | tf_op jit(solution)/shard_map/all_gather | solution.py:13
  313.6 2.5 reshape.2
  316.1 0.0 copy-done
  316.1 8.3 %fusion.7 = f32[2,512,768]{2,1,0:T(8,128)} fusion(f32[2,512,512]{2,1,0:T(8,128)S(1)} %copy-done, f32[768,512,1]{1,0,2:T(8,128)} %reshape.2), kind=kOutput, calls=%fused_computation.6 | convolution fusion | flops 4831838208 | bytes 6815744 | tf_op jit(solution)/shard_map/prl,li->pri/dot_general | solution.py:10
  324.4 0.0 all-reduce.3.cloned.1.call-update
  324.5 1.3 dynamic-slice
  326.4 101.2 %all-reduce.3.cloned.1.call-done = f32[2,512,768]{2,1,0:T(8,128)} async-done(((f32[2,512,768]{2,1,0:T(8,128)}), f32[2,512,768]{2,1,0:T(8,128)}) %all-reduce.3.cloned.1.call-update) | async-done | bytes 3145744 | tf_op jit(solution)/shard_map/psum | solution.py:16
  427.5 2.8 fusion.2
  430.3 307.2 %all-reduce = f32[256,32]{1,0:T(8,128)S(1)} all-reduce(f32[256,32]{1,0:T(8,128)S(1)} %fusion.2), channel_id=2, replica_groups=mesh['aux'=64,'basis'=8] {'aux'}, use_global_device_ids=true, to_apply=%region_1.0.clone | all-reduce | flops 8192 | bytes 65536
  737.5 0.6 constant_dynamic-slice_fusion
Async XLA Ops:
  6.5 309.6 %copy-start = (f32[2,512,512]{2,1,0:T(8,128)S(1)}, f32[2,512,512]{2,1,0:T(8,128)}, u32[]{:S(2)}) copy-start(f32[2,512,512]{2,1,0:T(8,128)} %param.2) | copy-start | bytes 6291460
  6.5 307.1 %all-gather.3.cloned.1.call-start = ((), (), s32[]{:S(2)}) async-start(), calls=%async_computation.1 | async-start | bytes 2129920 | tf_op jit(solution)/shard_map/all_gather | solution.py:13
  7.3 420.3 %all-reduce.3.cloned.1.call-start = ((), (), s32[]{:S(2)}) async-start(), calls=%async_computation | async-start | bytes 6291456 | tf_op jit(solution)/shard_map/psum | solution.py:16
Sparse Core Ops, SparseCore 0:
  9.4 304.1 all-gather.2
  324.6 102.9 all-reduce.2
where the time goes:
time: 745 us
  waiting for transfers between devices  408 us (55%)
  blocking collectives  307 us (41%)
  between operations  14.1 us (2%)
  matrix products  11.1 us (1%)
    unnamed x1, blocking collectives  307 us
    all_gather x1, waiting for transfers between devices, body(): lax.all_gather(occupied, 'aux', axis=1, tiled=True)  306 us
    psum x1, waiting for transfers between devices, body(): summed = lax.psum(partial_x, 'basis')  101 us
  transfers between devices with their start and end apart: 2, of which 2 were waited for; matrix products, arithmetic and copies ran while one was open for 0% of the time, Pallas kernels for 0%

commit v1 on v0

v1 whole, which is shorter than its diff:
```python
import jax
import jax.numpy as jnp
from jax import lax
from jax.sharding import Mesh
from jax.sharding import PartitionSpec as P

Y, X, ZL, ZH, C = 8, 4, 2, 4, 2


def spread(block, axes, count):
    return lax.all_to_all(
        jnp.broadcast_to(block, (count,) + block.shape), axes, 0, 0, tiled=True
    )


def body(integrals, occupied):
    parts, rows, depth = integrals.shape
    own = occupied.shape[1]
    half = rows // 2
    swapped = lax.ppermute(integrals, "c", [(0, 1), (1, 0)])
    core = lax.axis_index("c")
    low = jnp.where(core == 0, integrals, swapped)
    high = jnp.where(core == 0, swapped, integrals)

    coefficients = occupied.T.reshape(C, own // C, depth)
    sent = jnp.broadcast_to(coefficients, (Y, ZL) + coefficients.shape)
    sent = sent.reshape(Y * ZL * C, own // C, depth)
    near = lax.all_to_all(sent, ("y", "zl", "c"), 0, 0, tiled=True)
    whole = spread(near, "x", X)
    whole = whole.reshape(X * Y * ZL, C, own // C, depth)

    def term(block, c):
        return jnp.einsum(
            "gil,prl->gipr", whole[:, c], block, precision=lax.Precision.HIGH
        )

    partial_x = term(low, 0) + term(high, 1)
    orbitals = X * Y * ZL * own // C
    partial_x = partial_x.reshape(ZH, orbitals // ZH, parts, rows)
    arrived = lax.all_to_all(partial_x, "zh", 0, 0, tiled=True)
    summed = jnp.sum(arrived, axis=0)
    tile = jnp.einsum(
        "ipm,ipn->mn", summed[:, :, :half], summed[:, :, half:], precision=lax.Precision.HIGH
    )

    m, n = half // (Y * X * ZL), half // (ZH * C)
    tile = tile.reshape(Y, X, ZL, m, ZH, C, n).transpose(1, 2, 5, 0, 4, 3, 6)
    tile = lax.all_to_all(
        tile.reshape(X * ZL * C, Y, ZH, m, n), ("x", "zl", "c"), 0, 0, tiled=True
    )
    tile = jnp.sum(tile, axis=0).reshape(Y * ZH, m, n)
    tile = lax.all_to_all(tile, ("y", "zh"), 0, 0, tiled=True)
    return jnp.sum(tile, axis=0)


def solution(mesh):
    refined = Mesh(mesh.devices.reshape(Y, X, ZL, ZH, C), ("y", "x", "zl", "zh", "c"))
    aux, basis = ("y", "x", "zl"), ("zh", "c")
    return jax.shard_map(
        body,
        mesh=refined,
        in_specs=(P(aux, None, basis), P(basis, aux)),
        out_specs=P(aux, basis),
        check_vma=False,
    )
```

time: 745 us -> 151 us (0.20)
  the two profiles are of different devices: /device:TPU:32 before, /device:TPU:1 now
where the time goes in v1:
time: 151 us; the launch traced here: 150 us
  blocking collectives  75.4 us (50%)
  waiting for transfers between devices  33.8 us (22%)
  starting transfers between devices  17 us (11%)
  local copies, waits for them, and re-layouts  16.9 us (11%)
  other arithmetic  3.56 us (2%)
  matrix products  3.53 us (2%)
    all_to_all x1, blocking collectives, body(): arrived = lax.all_to_all(partial_x, 'zh', 0, 0, tiled=True)  36.8 us
    all_to_all x1, blocking collectives, body(): lax.all_to_all(tile.reshape(X * ZL * C, Y, ZH, m, n), ('x', 'zl', 'c'), 0...  22.5 us
    all_to_all x1, waiting for transfers between devices, spread(): lax.all_to_all(jnp.broadcast_to(block, (count,) + block.shape), axes, 0,...  19.2 us
    all_to_all x1, blocking collectives, body(): tile = lax.all_to_all(tile, ('y', 'zh'), 0, 0, tiled=True)  16.1 us
    all_to_all x1, waiting for transfers between devices, body(): near = lax.all_to_all(sent, ('y', 'zl', 'c'), 0, 0, tiled=True)  14.6 us
    all_to_all x1, starting transfers between devices, body(): near = lax.all_to_all(sent, ('y', 'zl', 'c'), 0, 0, tiled=True)  10.6 us
    all_to_all x1, starting transfers between devices, spread(): lax.all_to_all(jnp.broadcast_to(block, (count,) + block.shape), axes, 0,...  4.33 us
    slice x1, local copies, waits for them, and re-layouts, term(): whole[:, c]  3.52 us
  transfers between devices with their start and end apart: 3, of which 2 were waited for; matrix products, arithmetic and copies ran while one was open for 7% of the time, Pallas kernels for 0%

profile of v1, /device:TPU:1, one launch (start us, length us, event | category | flops | bytes accessed | tf_op | source)
XLA Modules:
  0.0 150.4 jit_solution(11400933287283784395)
XLA Ops:
  0.0 0.8 reshape.21
  0.8 0.8 broadcast_in_dim.6
  1.6 10.6 %all-to-all-start = ((f32[32,6,512]{2,1,0:T(8,128)}), f32[32,6,512]{2,1,0:T(8,128)S(1)}, u32[]{:S(2)}, u32[]{:S(2)}) async-start(f32[32,6,512]{2,1,0:T(8,128)} %bitcast.3), calls=%async_computation | async-start | bytes 1048576 | tf_op jit(solution)/shard_map/all_to_all | solution.py:28
  12.2 2.1 %collective-permute-start = (f32[2,512,512]{2,1,0:T(8,128)}, f32[2,512,512]{2,1,0:T(8,128)S(1)}, u32[]{:S(2)}, u32[]{:S(2)}) collective-permute-start(f32[2,512,512]{2,1,0:T(8,128)} %param.2), channel_id=1, source_target_pairs={{0,1},{1,0},{2,3},{3,2},{4,5},{5,4},{6,7},{7,6},{8,9},{9,8},{10,11... | collective-permute-start | bytes 6291464 | tf_op jit(solution)/shard_map/ppermute | solution.py:20
  14.3 14.6 %all-to-all-done = f32[32,6,512]{2,1,0:T(8,128)S(1)} async-done(((f32[32,6,512]{2,1,0:T(8,128)}), f32[32,6,512]{2,1,0:T(8,128)S(1)}, u32[]{:S(2)}, u32[]{:S(2)}) %all-to-all-start) | async-done | bytes 393248 | tf_op jit(solution)/shard_map/all_to_all | solution.py:28
  28.9 0.2 copy.25
  29.1 1.3 broadcast_in_dim.7
  30.5 4.3 %all-to-all-start.1 = ((f32[4,32,6,512]{3,1,2,0:T(8,128)}), f32[4,32,6,512]{3,1,2,0:T(8,128)}, u32[]{:S(2)}, u32[]{:S(2)}) async-start(f32[4,32,6,512]{3,1,2,0:T(8,128)} %broadcast_in_dim.7), calls=%async_computation.1 | async-start | bytes 3145728 | tf_op jit(solution)/shard_map/all_to_all | solution.py:11
  34.8 19.2 %all-to-all-done.1 = f32[4,32,6,512]{3,1,2,0:T(8,128)} async-done(((f32[4,32,6,512]{3,1,2,0:T(8,128)}), f32[4,32,6,512]{3,1,2,0:T(8,128)}, u32[]{:S(2)}, u32[]{:S(2)}) %all-to-all-start.1) | async-done | bytes 1572896 | tf_op jit(solution)/shard_map/all_to_all | solution.py:11
  54.1 2.7 %copy.26 = f32[4,32,6,512]{3,1,0,2:T(8,128)} copy(f32[4,32,6,512]{3,1,2,0:T(8,128)} %all-to-all-done.1) | data formatting | bytes 3145728 | tf_op jit(solution)/shard_map/all_to_all | solution.py:11
  56.8 3.0 %reshape.23 = f32[64,2,6,512]{3,1,0,2:T(2,128)} reshape(f32[4,32,6,512]{3,1,0,2:T(8,128)} %copy.26) | data formatting | bytes 3145728 | tf_op jit(solution)/shard_map/reshape | solution.py:30
  59.8 0.0 copy-start
  59.8 3.5 %fusion.12 = (f32[64,1,6,512]{3,1,0,2:T(1,128)S(1)}, f32[64,1,6,512]{3,1,0,2:T(1,128)S(1)}) fusion(f32[64,2,6,512]{3,1,0,2:T(2,128)} %reshape.23), kind=kLoop, calls=%fused_computation.14 | loop fusion | bytes 3145728 | tf_op jit(solution)/shard_map/slice | solution.py:34
  63.4 0.0 collective-permute-done
  63.4 0.0 copy-done
  63.4 1.5 %fusion = f32[2,512,64,6]{1,2,3,0:T(8,128)S(1)} fusion(f32[2,512,512]{2,1,0:T(8,128)S(1)} %collective-permute-done, f32[2,512,512]{2,1,0:T(8,128)S(1)} %copy-done, pred[]{:T(512)S(6)} %eq.4, f32[64,1,6,512]{3,1,0,2:T(1,128)S(1)} %get-tuple-element.6), kind=kOutput, calls=%fused_computation | convolution fusion | flops 1208483840 | bytes 6553601 | tf_op jit(solution)/shard_map/gil,prl->gipr/dot_general | solution.py:33
  64.9 1.6 %add_bitcast_fusion = f32[64,6,2,512]{3,0,1,2:T(8,128)S(1)} fusion(f32[2,512,64,6]{1,2,3,0:T(8,128)S(1)} %fusion, f32[2,512,512]{2,1,0:T(8,128)S(1)} %copy-done, f32[2,512,512]{2,1,0:T(8,128)S(1)} %collective-permute-done, pred[]{:T(512)S(6)} %eq.4, f32[64,1,6,512]{3,1,0,2:T(1,128)S(1)} %get-tuple-element.5), kind=kOutput, calls=%fused_computation.6 | convolution fusion | flops 1208877056 | bytes 8126465 | tf_op jit(solution)/shard_map/gil,prl->gipr/dot_general | solution.py:33
  66.5 1.2 copy.29
  67.7 36.8 %all_to_all.25 = f32[4,96,2,512]{3,2,1,0:T(2,128)S(1)} all-to-all(f32[4,96,2,512]{3,2,1,0:T(2,128)S(1)} %bitcast.38), channel_id=1, replica_groups=mesh['y'=8,'x'=4,'zl'=2,'zh'=4,'c'=2] {'zh'}, dimensions={0} | all-to-all | bytes 3145728 | tf_op jit(solution)/shard_map/all_to_all | solution.py:40
  104.5 0.9 reduce_sum.27
  105.4 0.1 fusion.13
  105.6 0.4 convolution_bitcast_fusion
  106.0 0.9 reshape.25
  106.9 0.6 copy.32
  107.5 0.5 reshape.33
  108.0 22.5 %all_to_all.26 = f32[16,1,4096]{2,1,0:T(1,128)S(1)} all-to-all(f32[16,1,4096]{2,1,0:T(1,128)S(1)} %reshape.33), channel_id=1, replica_groups=mesh['y'=8,'x'=4,'zl'=2,'zh'=4,'c'=2] {'x','zl','c'}, dimensions={0} | all-to-all | bytes 524288 | tf_op jit(solution)/shard_map/all_to_all | solution.py:48
  130.4 0.5 broadcast
  130.9 1.3 reduce
  132.2 0.3 reshape.34
  132.6 0.1 bitcast_reduce_fusion
  132.8 0.1 reshape.35
  132.9 16.1 %all_to_all.27 = f32[32,1,128]{2,1,0:T(1,128)S(1)} all-to-all(f32[32,1,128]{2,1,0:T(1,128)S(1)} %reshape.35), channel_id=1, replica_groups=mesh['y'=8,'x'=4,'zl'=2,'zh'=4,'c'=2] {'y','zh'}, dimensions={0} | all-to-all | bytes 32768 | tf_op jit(solution)/shard_map/all_to_all | solution.py:52
  149.0 0.7 reduce.1
  149.7 0.1 reshape.36
  149.8 0.6 reduce_sum.29
  (2 shorter events, 0.1 us)
Async XLA Ops:
  1.6 27.3 %all-to-all-start = ((f32[32,6,512]{2,1,0:T(8,128)}), f32[32,6,512]{2,1,0:T(8,128)S(1)}, u32[]{:S(2)}, u32[]{:S(2)}) async-start(f32[32,6,512]{2,1,0:T(8,128)} %bitcast.3), calls=%async_computation | async-start | bytes 1048576 | tf_op jit(solution)/shard_map/all_to_all | solution.py:28
  12.2 51.2 %collective-permute-start = (f32[2,512,512]{2,1,0:T(8,128)}, f32[2,512,512]{2,1,0:T(8,128)S(1)}, u32[]{:S(2)}, u32[]{:S(2)}) collective-permute-start(f32[2,512,512]{2,1,0:T(8,128)} %param.2), channel_id=1, source_target_pairs={{0,1},{1,0},{2,3},{3,2},{4,5},{5,4},{6,7},{7,6},{8,9},{9,8},{10,11... | collective-permute-start | bytes 6291464 | tf_op jit(solution)/shard_map/ppermute | solution.py:20
  30.5 23.6 %all-to-all-start.1 = ((f32[4,32,6,512]{3,1,2,0:T(8,128)}), f32[4,32,6,512]{3,1,2,0:T(8,128)}, u32[]{:S(2)}, u32[]{:S(2)}) async-start(f32[4,32,6,512]{3,1,2,0:T(8,128)} %broadcast_in_dim.7), calls=%async_computation.1 | async-start | bytes 3145728 | tf_op jit(solution)/shard_map/all_to_all | solution.py:11
  59.8 3.5 %copy-start = (f32[2,512,512]{2,1,0:T(8,128)S(1)}, f32[2,512,512]{2,1,0:T(8,128)}, u32[]{:S(2)}) copy-start(f32[2,512,512]{2,1,0:T(8,128)} %param.2) | copy-start | bytes 6291460

commit v2 on v1

v2 whole, which is shorter than its diff:
```python
import jax
import jax.numpy as jnp
from jax import lax
from jax.sharding import Mesh
from jax.sharding import PartitionSpec as P

Y, X, ZL, ZH, C = 8, 4, 2, 4, 2
LANES = 128


def body(integrals, occupied):
    parts, rows, depth = integrals.shape
    own = occupied.shape[1]
    half = rows // 2
    share = own // C
    swapped = lax.ppermute(integrals, "c", [(0, 1), (1, 0)])
    held = jnp.concatenate([integrals, swapped], axis=2).reshape(parts * rows, C * depth)

    sent = jnp.broadcast_to(
        occupied.T.reshape(C, share * depth // LANES, LANES),
        (Y, C, share * depth // LANES, LANES),
    )
    near = lax.all_to_all(
        sent.reshape(Y * C, -1, LANES), ("y", "c"), 0, 0, tiled=True
    ).reshape(Y, C, share, depth)
    near = jnp.where(lax.axis_index("c") == 0, near, near[:, ::-1])
    near = near.transpose(0, 2, 1, 3).reshape(Y * share, C * depth)
    whole = lax.all_to_all(
        jnp.broadcast_to(near, (X * ZL,) + near.shape), ("x", "zl"), 0, 0, tiled=True
    )
    whole = whole.reshape(-1, C * depth)

    partial_x = lax.dot_general(
        whole, held, (((1,), (1,)), ((), ())), precision=lax.Precision.HIGH
    )
    orbitals = partial_x.shape[0] // ZH
    arrived = lax.all_to_all(
        partial_x.reshape(ZH, orbitals, parts * rows), "zh", 0, 0, tiled=True
    )
    summed = jnp.sum(arrived, axis=0)
    tile = sum(
        lax.dot_general(
            summed[:, p * rows : p * rows + half],
            summed[:, p * rows + half : (p + 1) * rows],
            (((0,), (0,)), ((), ())),
            precision=lax.Precision.HIGHEST,
        )
        for p in range(parts)
    )

    m, n = half // (Y * X * ZL), half // (ZH * C)
    tile = lax.all_to_all(tile.reshape(Y * X, ZL * m, half), ("y", "x"), 0, 0, tiled=True)
    tile = jnp.sum(tile, axis=0).reshape(ZL, m, ZH * C, n).transpose(0, 2, 1, 3)
    tile = lax.all_to_all(
        tile.reshape(ZL * ZH * C, m * n), ("zl", "zh", "c"), 0, 0, tiled=True
    )
    return jnp.sum(tile, axis=0).reshape(m, n)


def solution(mesh):
    refined = Mesh(mesh.devices.reshape(Y, X, ZL, ZH, C), ("y", "x", "zl", "zh", "c"))
    aux, basis = ("y", "x", "zl"), ("zh", "c")
    return jax.shard_map(
        body,
        mesh=refined,
        in_specs=(P(aux, None, basis), P(basis, aux)),
        out_specs=P(aux, basis),
        check_vma=False,
    )
```

time: 151 us -> 131 us (0.87)
  local copies, waits for them, and re-layouts: 16.9 us -> 3.86 us
  waiting for transfers between devices: 33.8 us -> 26 us
  matrix products: 3.53 us -> 5.6 us
    all_to_all x2, waiting for transfers between devices: 33.8 us -> 21.7 us  [the longest x1 11.3 us: body(): lax.all_to_all(jnp.broadcast_to(near, (X * ZL,) + near.shape), ('x', 'zl'...]
    ppermute x1, waiting for transfers between devices: 0.01 us -> 4.34 us  [body(): swapped = lax.ppermute(integrals, 'c', [(0, 1), (1, 0)])]
    concatenate x0 -> x1, other arithmetic: none -> 3.96 us  [body(): jnp.concatenate([integrals, swapped], axis=2)]
    reshape x5 -> x4, local copies, waits for them, and re-layouts: 5.3 us -> 1.53 us  [the longest x1 0.76 us: body(): occupied.T.reshape(C, share * depth // LANES, LANES)]
    slice x2 -> x0, local copies, waits for them, and re-layouts: 3.66 us -> none  [the longest x1 3.52 us: term(): whole[:, c]]
    all_to_all x3 -> x1, local copies, waits for them, and re-layouts: 3.49 us -> 0.08 us  [body(): lax.all_to_all(tile.reshape(ZL * ZH * C, m * n), ('zl', 'zh', 'c'), 0, 0,...]
    dot_general x3, matrix products: 3.53 us -> 5.6 us  [the longest x1 4.77 us: body(): lax.dot_general(whole, held, (((1,), (1,)), ((), ())), precision=lax.Prec...]
    all_to_all x2 -> x0, other arithmetic: 1.94 us -> none  [the longest x1 1.26 us: body(): lax.all_to_all(tile.reshape(X * ZL * C, Y, ZH, m, n), ('x', 'zl', 'c'), 0...]
  transfers between devices with their start and end apart: 3 -> 3, of which waited for: 2 -> 3; matrix products, arithmetic and copies ran while one was open for 7% -> 3% of each run, Pallas kernels for 0% -> 0%
where the time goes in v2:
time: 131 us
  blocking collectives  74.5 us (57%)
  waiting for transfers between devices  26 us (20%)
  starting transfers between devices  16.3 us (12%)
  matrix products  5.6 us (4%)
  other arithmetic  4.17 us (3%)
  local copies, waits for them, and re-layouts  3.86 us (3%)
    all_to_all x1, blocking collectives, body(): lax.all_to_all(partial_x.reshape(ZH, orbitals, parts * rows), 'zh', 0, 0,...  46.3 us
    all_to_all x1, blocking collectives, body(): lax.all_to_all(tile.reshape(ZL * ZH * C, m * n), ('zl', 'zh', 'c'), 0, 0,...  14.6 us
    all_to_all x1, blocking collectives, body(): lax.all_to_all(tile.reshape(Y * X, ZL * m, half), ('y', 'x'), 0, 0, tiled...  13.6 us
    all_to_all x1, waiting for transfers between devices, body(): lax.all_to_all(jnp.broadcast_to(near, (X * ZL,) + near.shape), ('x', 'zl'...  11.3 us
    all_to_all x1, waiting for transfers between devices, body(): lax.all_to_all(sent.reshape(Y * C, -1, LANES), ('y', 'c'), 0, 0, tiled=True)  10.4 us
    all_to_all x1, starting transfers between devices, body(): lax.all_to_all(sent.reshape(Y * C, -1, LANES), ('y', 'c'), 0, 0, tiled=True)  10.2 us
    dot_general x1, matrix products, body(): lax.dot_general(whole, held, (((1,), (1,)), ((), ())), precision=lax.Prec...  4.77 us
    ppermute x1, waiting for transfers between devices, body(): swapped = lax.ppermute(integrals, 'c', [(0, 1), (1, 0)])  4.34 us
  transfers between devices with their start and end apart: 3, of which 3 were waited for; matrix products, arithmetic and copies ran while one was open for 3% of the time, Pallas kernels for 0%

profile of v2, /device:TPU:1, one launch (start us, length us, event | category | flops | bytes accessed | tf_op | source)
XLA Modules:
  0.0 130.6 jit_solution(13431892899995324578)
XLA Ops:
  0.0 0.8 reshape.32
  0.8 0.7 broadcast_in_dim.6
  1.4 10.2 %all-to-all-start = ((f32[16,24,128]{2,1,0:T(8,128)}), f32[16,24,128]{2,1,0:T(8,128)S(1)}, u32[]{:S(2)}, u32[]{:S(2)}) async-start(f32[16,24,128]{2,1,0:T(8,128)} %bitcast.1), calls=%async_computation | async-start | bytes 393216 | tf_op jit(solution)/shard_map/all_to_all | solution.py:23
  11.6 10.4 %all-to-all-done = f32[16,24,128]{2,1,0:T(8,128)S(1)} async-done(((f32[16,24,128]{2,1,0:T(8,128)}), f32[16,24,128]{2,1,0:T(8,128)S(1)}, u32[]{:S(2)}, u32[]{:S(2)}) %all-to-all-start) | async-done | bytes 196640 | tf_op jit(solution)/shard_map/all_to_all | solution.py:23
  22.1 0.2 copy.5
  22.3 1.4 %broadcast_in_dim.7 = f32[8,48,1024]{2,1,0:T(8,128)} broadcast(f32[48,1024]{1,0:T(8,128)S(1)} %bitcast.20), dimensions={1,2} | broadcast | bytes 1769472 | tf_op jit(solution)/shard_map/broadcast_in_dim | solution.py:29
  23.6 4.2 %all-to-all-start.1 = ((f32[8,48,1024]{2,1,0:T(8,128)}), f32[8,48,1024]{2,1,0:T(8,128)S(1)}, u32[]{:S(2)}, u32[]{:S(2)}) async-start(f32[8,48,1024]{2,1,0:T(8,128)} %broadcast_in_dim.7), calls=%async_computation.1 | async-start | bytes 3145728 | tf_op jit(solution)/shard_map/all_to_all | solution.py:28
  27.9 1.9 %collective-permute-start = (f32[2,512,512]{2,1,0:T(8,128)}, f32[2,512,512]{2,1,0:T(8,128)S(1)}, u32[]{:S(2)}, u32[]{:S(2)}) collective-permute-start(f32[2,512,512]{2,1,0:T(8,128)} %param.2), channel_id=1, source_target_pairs={{0,1},{1,0},{2,3},{3,2},{4,5},{5,4},{6,7},{7,6},{8,9},{9,8},{10,11... | collective-permute-start | bytes 6291464 | tf_op jit(solution)/shard_map/ppermute | solution.py:16
  29.8 4.3 %collective-permute-done = f32[2,512,512]{2,1,0:T(8,128)S(1)} collective-permute-done((f32[2,512,512]{2,1,0:T(8,128)}, f32[2,512,512]{2,1,0:T(8,128)S(1)}, u32[]{:S(2)}, u32[]{:S(2)}) %collective-permute-start) | collective-permute-done | bytes 2097184 | tf_op jit(solution)/shard_map/ppermute | solution.py:16
  34.1 4.0 %pad_maximum_fusion = f32[2,512,1024]{2,1,0:T(8,128)} fusion(f32[2,512,512]{2,1,0:T(8,128)S(1)} %collective-permute-done, f32[2,512,512]{2,1,0:T(8,128)} %param.2), kind=kLoop, calls=%fused_computation | loop fusion | flops 1048576 | bytes 8388608 | tf_op jit(solution)/shard_map/concatenate | solution.py:17
  38.1 11.3 %all-to-all-done.1 = f32[8,48,1024]{2,1,0:T(8,128)S(1)} async-done(((f32[8,48,1024]{2,1,0:T(8,128)}), f32[8,48,1024]{2,1,0:T(8,128)S(1)}, u32[]{:S(2)}, u32[]{:S(2)}) %all-to-all-start.1) | async-done | bytes 1572896 | tf_op jit(solution)/shard_map/all_to_all | solution.py:28
  49.4 4.8 %fusion.7 = f32[4,96,1024]{2,1,0:T(8,128)S(1)} fusion(f32[4,96,1024]{2,1,0:T(8,128)S(1)} %bitcast.18, f32[1024,1024,1]{1,0,2:T(8,128)} %bitcast.17), kind=kOutput, calls=%fused_computation.10 | convolution fusion | flops 2415919104 | bytes 7340032 | tf_op jit(solution)/shard_map/dot_general | solution.py:33
  54.2 46.3 %all_to_all.29 = f32[4,96,1024]{2,1,0:T(8,128)S(1)} all-to-all(f32[4,96,1024]{2,1,0:T(8,128)S(1)} %fusion.7), channel_id=1, replica_groups=mesh['y'=8,'x'=4,'zl'=2,'zh'=4,'c'=2] {'zh'}, dimensions={0} | all-to-all | bytes 3145728 | tf_op jit(solution)/shard_map/all_to_all | solution.py:37
  100.5 0.1 reduce_sum.27
  100.6 0.4 fusion.4
  101.0 0.4 fusion
  101.4 13.6 %all_to_all.30 = f32[32,8,256]{2,1,0:T(8,128)S(1)} all-to-all(f32[32,8,256]{2,1,0:T(8,128)S(1)} %fusion), channel_id=1, replica_groups=mesh['y'=8,'x'=4,'zl'=2,'zh'=4,'c'=2] {'y','x'}, dimensions={0} | all-to-all | bytes 524288 | tf_op jit(solution)/shard_map/all_to_all | solution.py:52
  115.1 0.1 reshape.38
  115.1 0.1 all_to_all.22
  115.2 14.6 %all_to_all.31 = f32[16,1,128]{2,1,0:T(1,128)S(1)} all-to-all(f32[16,1,128]{2,1,0:T(1,128)S(1)} %bitcast.23), channel_id=1, replica_groups=mesh['y'=8,'x'=4,'zl'=2,'zh'=4,'c'=2] {'zl','zh','c'}, dimensions={0} | all-to-all | bytes 16384 | tf_op jit(solution)/shard_map/all_to_all | solution.py:54
  129.9 0.7 reshape.39
  (6 shorter events, 0.2 us)
Async XLA Ops:
  1.4 20.6 %all-to-all-start = ((f32[16,24,128]{2,1,0:T(8,128)}), f32[16,24,128]{2,1,0:T(8,128)S(1)}, u32[]{:S(2)}, u32[]{:S(2)}) async-start(f32[16,24,128]{2,1,0:T(8,128)} %bitcast.1), calls=%async_computation | async-start | bytes 393216 | tf_op jit(solution)/shard_map/all_to_all | solution.py:23
  23.6 25.7 %all-to-all-start.1 = ((f32[8,48,1024]{2,1,0:T(8,128)}), f32[8,48,1024]{2,1,0:T(8,128)S(1)}, u32[]{:S(2)}, u32[]{:S(2)}) async-start(f32[8,48,1024]{2,1,0:T(8,128)} %broadcast_in_dim.7), calls=%async_computation.1 | async-start | bytes 3145728 | tf_op jit(solution)/shard_map/all_to_all | solution.py:28
  27.9 6.3 %collective-permute-start = (f32[2,512,512]{2,1,0:T(8,128)}, f32[2,512,512]{2,1,0:T(8,128)S(1)}, u32[]{:S(2)}, u32[]{:S(2)}) collective-permute-start(f32[2,512,512]{2,1,0:T(8,128)} %param.2), channel_id=1, source_target_pairs={{0,1},{1,0},{2,3},{3,2},{4,5},{5,4},{6,7},{7,6},{8,9},{9,8},{10,11... | collective-permute-start | bytes 6291464 | tf_op jit(solution)/shard_map/ppermute | solution.py:16

commit v3 on v2

--- a/solution.py
+++ b/solution.py
@@ -16,28 +16,43 @@
     swapped = lax.ppermute(integrals, "c", [(0, 1), (1, 0)])
     held = jnp.concatenate([integrals, swapped], axis=2).reshape(parts * rows, C * depth)
 
+    pairs = [((x + d + 2) % X * ZH + d, x * ZH + d) for x in range(X) for d in range(ZH)]
+    moved = lax.ppermute(occupied.T, ("x", "zh"), pairs)
     sent = jnp.broadcast_to(
-        occupied.T.reshape(C, share * depth // LANES, LANES),
-        (Y, C, share * depth // LANES, LANES),
+        moved.reshape(C, share * depth // LANES, LANES),
+        (Y, ZL, C, share * depth // LANES, LANES),
     )
     near = lax.all_to_all(
-        sent.reshape(Y * C, -1, LANES), ("y", "c"), 0, 0, tiled=True
-    ).reshape(Y, C, share, depth)
+        sent.reshape(Y * ZL * C, -1, LANES), ("y", "zl", "c"), 0, 0, tiled=True
+    ).reshape(Y * ZL, C, share, depth)
     near = jnp.where(lax.axis_index("c") == 0, near, near[:, ::-1])
-    near = near.transpose(0, 2, 1, 3).reshape(Y * share, C * depth)
-    whole = lax.all_to_all(
-        jnp.broadcast_to(near, (X * ZL,) + near.shape), ("x", "zl"), 0, 0, tiled=True
+    near = near.transpose(0, 2, 1, 3).reshape(Y * ZL * share, C * depth)
+
+    def fetch(source, step):
+        return lax.ppermute(source, "x", [((x + step) % X, x) for x in range(X)])
+
+    def term(block):
+        return lax.dot_general(
+            block, held, (((1,), (1,)), ((), ())), precision=lax.Precision.HIGH
+        )
+
+    up = [(d, (d + 1) % ZH) for d in range(ZH)]
+    down = [(d, (d - 1) % ZH) for d in range(ZH)]
+    next_one, last_one = fetch(near, -1), fetch(near, 1)
+    opposite = term(near)
+    cut = opposite.shape[0] // 2
+    from_below = lax.ppermute(opposite[:cut], "zh", up)
+    from_above = lax.ppermute(opposite[cut:], "zh", down)
+    above, below = term(next_one), term(last_one)
+    near, above = lax.optimization_barrier((near, above))
+    arrived_up = lax.ppermute(
+        jnp.concatenate([above[:cut] + from_below, above[cut:]]), "zh", up
     )
-    whole = whole.reshape(-1, C * depth)
-
-    partial_x = lax.dot_general(
-        whole, held, (((1,), (1,)), ((), ())), precision=lax.Precision.HIGH
+    arrived_down = lax.ppermute(
+        jnp.concatenate([below[:cut], below[cut:] + from_above]), "zh", down
     )
-    orbitals = partial_x.shape[0] // ZH
-    arrived = lax.all_to_all(
-        partial_x.reshape(ZH, orbitals, parts * rows), "zh", 0, 0, tiled=True
-    )
-    summed = jnp.sum(arrived, axis=0)
+    mine = lax.optimization_barrier(term(fetch(near, 2)))
+    summed = mine + arrived_up + arrived_down
     tile = sum(
         lax.dot_general(
             summed[:, p * rows : p * rows + half],

time: 131 us -> 126 us (0.962)
  blocking collectives: 74.5 us -> 46 us
  starting transfers between devices: 16.3 us -> 43.2 us
  matrix products: 5.6 us -> 9.6 us
  waiting for transfers between devices: 26 us -> 22.1 us
  other arithmetic: 4.17 us -> 2.34 us
  local copies, waits for them, and re-layouts: 3.86 us -> 2.09 us
    all_to_all x1 -> x0, blocking collectives: 46.3 us -> none  [body(): lax.all_to_all(partial_x.reshape(ZH, orbitals, parts * rows), 'zh', 0, 0,...]
    ppermute x0 -> x8, starting transfers between devices: none -> 29.4 us  [the longest x3 8.63 us: fetch(): return lax.ppermute(source, 'x', [((x + step) % X, x) for x in range(X)])]
    all_to_all x1, blocking collectives: 13.6 us -> 30.1 us  [body(): lax.all_to_all(tile.reshape(Y * X, ZL * m, half), ('y', 'x'), 0, 0, tiled...]
    all_to_all x2 -> x1, starting transfers between devices: 14.4 us -> 4.85 us  [body(): lax.all_to_all(sent.reshape(Y * ZL * C, -1, LANES), ('y', 'zl', 'c'), 0,...]
    ppermute x0 -> x8, waiting for transfers between devices: none -> 8.29 us  [the longest x1 4.45 us: body(): moved = lax.ppermute(occupied.T, ('x', 'zh'), pairs)]
    all_to_all x2 -> x1, waiting for transfers between devices: 21.7 us -> 13.8 us  [body(): lax.all_to_all(sent.reshape(Y * ZL * C, -1, LANES), ('y', 'zl', 'c'), 0,...]
    ppermute x1, starting transfers between devices: 1.91 us -> 8.91 us  [body(): swapped = lax.ppermute(integrals, 'c', [(0, 1), (1, 0)])]
    ppermute x1, waiting for transfers between devices: 4.34 us -> 0.01 us  [body(): swapped = lax.ppermute(integrals, 'c', [(0, 1), (1, 0)])]
  transfers between devices with their start and end apart: 3 -> 10, of which waited for: 3 -> 5; matrix products, arithmetic and copies ran while one was open for 3% -> 10% of each run, Pallas kernels for 0% -> 0%
where the time goes in v3:
time: 126 us
  blocking collectives  46 us (37%)
  starting transfers between devices  43.2 us (34%)
  waiting for transfers between devices  22.1 us (18%)
  matrix products  9.6 us (8%)
  other arithmetic  2.34 us (2%)
  local copies, waits for them, and re-layouts  2.09 us (2%)
    all_to_all x1, blocking collectives, body(): lax.all_to_all(tile.reshape(Y * X, ZL * m, half), ('y', 'x'), 0, 0, tiled...  30.1 us
    all_to_all x1, blocking collectives, body(): lax.all_to_all(tile.reshape(ZL * ZH * C, m * n), ('zl', 'zh', 'c'), 0, 0,...  15.9 us
    all_to_all x1, waiting for transfers between devices, body(): lax.all_to_all(sent.reshape(Y * ZL * C, -1, LANES), ('y', 'zl', 'c'), 0,...  13.8 us
    ppermute x1, starting transfers between devices, body(): swapped = lax.ppermute(integrals, 'c', [(0, 1), (1, 0)])  8.91 us
    dot_general x4, matrix products, term(): lax.dot_general(block, held, (((1,), (1,)), ((), ())), precision=lax.Prec...  8.77 us
    ppermute x3, starting transfers between devices, fetch(): return lax.ppermute(source, 'x', [((x + step) % X, x) for x in range(X)])  8.63 us
    ppermute x1, starting transfers between devices, body(): from_above = lax.ppermute(opposite[cut:], 'zh', down)  5.96 us
    ppermute x1, starting transfers between devices, body(): from_below = lax.ppermute(opposite[:cut], 'zh', up)  5.52 us
  transfers between devices with their start and end apart: 10, of which 5 were waited for; matrix products, arithmetic and copies ran while one was open for 10% of the time, Pallas kernels for 0%

profile of v3, /device:TPU:1, one launch (start us, length us, event | category | flops | bytes accessed | tf_op | source)
XLA Modules:
  0.0 125.5 jit_solution(8369470972439139563)
XLA Ops:
  0.0 0.0 copy-start
  0.0 8.9 %collective-permute-start.2 = (f32[2,512,512]{2,1,0:T(8,128)}, f32[2,512,512]{2,1,0:T(8,128)}, u32[]{:S(2)}, u32[]{:S(2)}) collective-permute-start(f32[2,512,512]{2,1,0:T(8,128)} %param.2), channel_id=1, source_target_pairs={{0,1},{1,0},{2,3},{3,2},{4,5},{5,4},{6,7},{7,6},{8,9},{9,8},{10,11... | collective-permute-start | bytes 6291464 | tf_op jit(solution)/shard_map/ppermute | solution.py:16
  8.9 1.9 %collective-permute-start = (f32[12,512]{1,0:T(8,128)}, f32[12,512]{1,0:T(8,128)S(1)}, u32[]{:S(2)}, u32[]{:S(2)}) collective-permute-start(f32[12,512]{1,0:T(8,128)} %bitcast.31), channel_id=1, source_target_pairs={{32,0},{50,2},{4,4},{22,6},{48,16},{2,18},{20,20},{38,22},{0,32},{... | collective-permute-start | bytes 73736 | tf_op jit(solution)/shard_map/ppermute | solution.py:20
  10.8 4.4 %collective-permute-done = f32[12,512]{1,0:T(8,128)S(1)} collective-permute-done((f32[12,512]{1,0:T(8,128)}, f32[12,512]{1,0:T(8,128)S(1)}, u32[]{:S(2)}, u32[]{:S(2)}) %collective-permute-start) | collective-permute-done | bytes 24608 | tf_op jit(solution)/shard_map/ppermute | solution.py:20
  15.3 0.8 broadcast_in_dim.3
  16.1 4.9 %all-to-all-start = ((f32[32,24,128]{2,1,0:T(8,128)}), f32[32,24,128]{2,1,0:T(8,128)S(1)}, u32[]{:S(2)}, u32[]{:S(2)}) async-start(f32[32,24,128]{2,1,0:T(8,128)} %bitcast.1), calls=%async_computation | async-start | bytes 786432 | tf_op jit(solution)/shard_map/all_to_all | solution.py:25
  20.9 13.8 %all-to-all-done = f32[32,24,128]{2,1,0:T(8,128)S(1)} async-done(((f32[32,24,128]{2,1,0:T(8,128)}), f32[32,24,128]{2,1,0:T(8,128)S(1)}, u32[]{:S(2)}, u32[]{:S(2)}) %all-to-all-start) | async-done | bytes 393248 | tf_op jit(solution)/shard_map/all_to_all | solution.py:25
  34.7 0.1 reshape.30
  34.8 0.3 copy.6
  35.1 0.1 copy.9
  35.2 3.1 %collective-permute-start.1 = (f32[96,1024]{1,0:T(8,128)S(1)}, f32[96,1024]{1,0:T(8,128)S(1)}, u32[]{:S(2)}, u32[]{:S(2)}) collective-permute-start(f32[96,1024]{1,0:T(8,128)S(1)} %bitcast.24), channel_id=1, source_target_pairs={{48,0},{0,16},{16,32},{32,48},{49,1},{1,17},{17,33},{33,49},{50,2}... | collective-permute-start | bytes 1179656 | tf_op jit(solution)/shard_map/ppermute | solution.py:32
  38.3 3.4 %collective-permute-start.6 = (f32[96,1024]{1,0:T(8,128)S(1)}, f32[96,1024]{1,0:T(8,128)S(1)}, u32[]{:S(2)}, u32[]{:S(2)}) collective-permute-start(f32[96,1024]{1,0:T(8,128)S(1)} %bitcast.25), channel_id=1, source_target_pairs={{16,0},{32,16},{48,32},{0,48},{17,1},{33,17},{49,33},{1,49},{18,2}... | collective-permute-start | bytes 1179656 | tf_op jit(solution)/shard_map/ppermute | solution.py:32
  41.7 0.0 collective-permute-done.2
  41.7 0.0 copy-done
  41.7 2.0 %pad_maximum_fusion = f32[2,512,1024]{2,1,0:T(8,128)S(1)} fusion(f32[2,512,512]{2,1,0:T(8,128)} %collective-permute-done.2, f32[2,512,512]{2,1,0:T(8,128)S(1)} %copy-done), kind=kLoop, calls=%fused_computation | loop fusion | flops 1048576 | bytes 8388608 | tf_op jit(solution)/shard_map/concatenate | solution.py:17
  43.8 2.2 %fusion.11 = f32[96,1024]{1,0:T(8,128)S(1)} fusion(f32[96,1024]{1,0:T(8,128)S(1)} %bitcast.26, f32[1024,1024]{1,0:T(8,128)S(1)} %bitcast.20), kind=kOutput, calls=%fused_computation.19 | convolution fusion | flops 603979776 | bytes 4980736 | tf_op jit(solution)/shard_map/dot_general | solution.py:35
  46.0 1.2 collective-permute-done.1
  47.2 2.2 %fusion.9 = f32[96,1024]{1,0:T(8,128)S(1)} fusion(f32[96,1024]{1,0:T(8,128)S(1)} %collective-permute-done.1, f32[1024,1024]{1,0:T(8,128)S(1)} %bitcast.21), kind=kOutput, calls=%fused_computation.17 | convolution fusion | flops 603979776 | bytes 4980736 | tf_op jit(solution)/shard_map/dot_general | solution.py:35
  49.5 5.5 %collective-permute-start.4 = (f32[48,1024]{1,0:T(8,128)S(1)}, f32[48,1024]{1,0:T(8,128)S(1)}, u32[]{:S(2)}, u32[]{:S(2)}) collective-permute-start(f32[48,1024]{1,0:T(8,128)S(1)} %get-tuple-element.11), channel_id=1, source_target_pairs={{0,2},{2,4},{4,6},{6,0},{1,3},{3,5},{5,7},{7,1},{8,10},{10,12},{12... | collective-permute-start | bytes 589832 | tf_op jit(solution)/shard_map/ppermute | solution.py:44
  55.0 6.0 %collective-permute-start.7 = (f32[48,1024]{1,0:T(8,128)S(1)}, f32[48,1024]{1,0:T(8,128)S(1)}, u32[]{:S(2)}, u32[]{:S(2)}) collective-permute-start(f32[48,1024]{1,0:T(8,128)S(1)} %get-tuple-element.12), channel_id=1, source_target_pairs={{0,6},{2,0},{4,2},{6,4},{1,7},{3,1},{5,3},{7,5},{8,14},{10,8},{12,... | collective-permute-start | bytes 589832 | tf_op jit(solution)/shard_map/ppermute | solution.py:45
  61.0 2.1 %collective-permute-start.3 = (f32[96,1024]{1,0:T(8,128)S(1)}, f32[96,1024]{1,0:T(8,128)S(1)}, u32[]{:S(2)}, u32[]{:S(2)}) collective-permute-start(f32[96,1024]{1,0:T(8,128)S(1)} %bitcast.27), channel_id=1, source_target_pairs={{32,0},{48,16},{0,32},{16,48},{33,1},{49,17},{1,33},{17,49},{34,2}... | collective-permute-start | bytes 1179656 | tf_op jit(solution)/shard_map/ppermute | solution.py:32
  63.1 0.0 collective-permute-done.6
  63.1 2.2 %fusion.12 = f32[96,1024]{1,0:T(8,128)S(1)} fusion(f32[96,1024]{1,0:T(8,128)S(1)} %collective-permute-done.6, f32[1024,1024]{1,0:T(8,128)S(1)} %bitcast.22), kind=kOutput, calls=%fused_computation.20 | convolution fusion | flops 603979776 | bytes 4980736 | tf_op jit(solution)/shard_map/dot_general | solution.py:35
  65.3 0.0 collective-permute-done.4
  65.4 1.9 %collective-permute-start.5 = (f32[96,1024]{1,0:T(8,128)S(1)}, f32[96,1024]{1,0:T(8,128)S(1)}, u32[]{:S(2)}, u32[]{:S(2)}) collective-permute-start(f32[96,1024]{1,0:T(8,128)S(1)} %pad_maximum_fusion.1), channel_id=1, source_target_pairs={{0,2},{2,4},{4,6},{6,0},{1,3},{3,5},{5,7},{7,1},{8,10},{10,12},{12... | collective-permute-start | bytes 1179656 | tf_op jit(solution)/shard_map/ppermute | solution.py:48
  67.3 0.0 collective-permute-done.7
  67.4 5.5 %collective-permute-start.8 = (f32[96,1024]{1,0:T(8,128)S(1)}, f32[96,1024]{1,0:T(8,128)S(1)}, u32[]{:S(2)}, u32[]{:S(2)}) collective-permute-start(f32[96,1024]{1,0:T(8,128)S(1)} %pad_maximum_fusion.2), channel_id=1, source_target_pairs={{0,6},{2,0},{4,2},{6,4},{1,7},{3,1},{5,3},{7,5},{8,14},{10,8},{12,... | collective-permute-start | bytes 1179656 | tf_op jit(solution)/shard_map/ppermute | solution.py:51
  72.9 0.0 collective-permute-done.3
  72.9 2.2 %fusion.10 = f32[96,1024]{1,0:T(8,128)S(1)} fusion(f32[96,1024]{1,0:T(8,128)S(1)} %collective-permute-done.3, f32[1024,1024]{1,0:T(8,128)S(1)} %bitcast.23), kind=kOutput, calls=%fused_computation.18 | convolution fusion | flops 603979776 | bytes 4980736 | tf_op jit(solution)/shard_map/dot_general | solution.py:35
  75.1 1.6 %collective-permute-done.5 = f32[96,1024]{1,0:T(8,128)S(1)} collective-permute-done((f32[96,1024]{1,0:T(8,128)S(1)}, f32[96,1024]{1,0:T(8,128)S(1)}, u32[]{:S(2)}, u32[]{:S(2)}) %collective-permute-start.5) | collective-permute-done | bytes 393248 | tf_op jit(solution)/shard_map/ppermute | solution.py:48
  76.8 0.9 collective-permute-done.8
  77.7 0.1 add_add_fusion
  77.8 0.4 fusion.2
  78.2 0.4 fusion
  78.6 30.1 %all_to_all.19 = f32[32,8,256]{2,1,0:T(8,128)S(1)} all-to-all(f32[32,8,256]{2,1,0:T(8,128)S(1)} %fusion), channel_id=1, replica_groups=mesh['y'=8,'x'=4,'zl'=2,'zh'=4,'c'=2] {'y','x'}, dimensions={0} | all-to-all | bytes 524288 | tf_op jit(solution)/shard_map/all_to_all | solution.py:67
  108.8 0.1 reshape.34
  108.8 0.1 all_to_all.14
  108.9 15.9 %all_to_all.20 = f32[16,1,128]{2,1,0:T(1,128)S(1)} all-to-all(f32[16,1,128]{2,1,0:T(1,128)S(1)} %bitcast.30), channel_id=1, replica_groups=mesh['y'=8,'x'=4,'zl'=2,'zh'=4,'c'=2] {'zl','zh','c'}, dimensions={0} | all-to-all | bytes 16384 | tf_op jit(solution)/shard_map/all_to_all | solution.py:69
  124.9 0.7 reshape.35
  (10 shorter events, 0.3 us)
Async XLA Ops:
  0.0 41.7 %copy-start = (f32[2,512,512]{2,1,0:T(8,128)S(1)}, f32[2,512,512]{2,1,0:T(8,128)}, u32[]{:S(2)}) copy-start(f32[2,512,512]{2,1,0:T(8,128)} %param.2) | copy-start | bytes 6291460
  0.0 41.7 %collective-permute-start.2 = (f32[2,512,512]{2,1,0:T(8,128)}, f32[2,512,512]{2,1,0:T(8,128)}, u32[]{:S(2)}, u32[]{:S(2)}) collective-permute-start(f32[2,512,512]{2,1,0:T(8,128)} %param.2), channel_id=1, source_target_pairs={{0,1},{1,0},{2,3},{3,2},{4,5},{5,4},{6,7},{7,6},{8,9},{9,8},{10,11... | collective-permute-start | bytes 6291464 | tf_op jit(solution)/shard_map/ppermute | solution.py:16
  8.9 6.4 %collective-permute-start = (f32[12,512]{1,0:T(8,128)}, f32[12,512]{1,0:T(8,128)S(1)}, u32[]{:S(2)}, u32[]{:S(2)}) collective-permute-start(f32[12,512]{1,0:T(8,128)} %bitcast.31), channel_id=1, source_target_pairs={{32,0},{50,2},{4,4},{22,6},{48,16},{2,18},{20,20},{38,22},{0,32},{... | collective-permute-start | bytes 73736 | tf_op jit(solution)/shard_map/ppermute | solution.py:20
  16.1 18.6 %all-to-all-start = ((f32[32,24,128]{2,1,0:T(8,128)}), f32[32,24,128]{2,1,0:T(8,128)S(1)}, u32[]{:S(2)}, u32[]{:S(2)}) async-start(f32[32,24,128]{2,1,0:T(8,128)} %bitcast.1), calls=%async_computation | async-start | bytes 786432 | tf_op jit(solution)/shard_map/all_to_all | solution.py:25
  35.2 12.0 %collective-permute-start.1 = (f32[96,1024]{1,0:T(8,128)S(1)}, f32[96,1024]{1,0:T(8,128)S(1)}, u32[]{:S(2)}, u32[]{:S(2)}) collective-permute-start(f32[96,1024]{1,0:T(8,128)S(1)} %bitcast.24), channel_id=1, source_target_pairs={{48,0},{0,16},{16,32},{32,48},{49,1},{1,17},{17,33},{33,49},{50,2}... | collective-permute-start | bytes 1179656 | tf_op jit(solution)/shard_map/ppermute | solution.py:32
  38.3 24.8 %collective-permute-start.6 = (f32[96,1024]{1,0:T(8,128)S(1)}, f32[96,1024]{1,0:T(8,128)S(1)}, u32[]{:S(2)}, u32[]{:S(2)}) collective-permute-start(f32[96,1024]{1,0:T(8,128)S(1)} %bitcast.25), channel_id=1, source_target_pairs={{16,0},{32,16},{48,32},{0,48},{17,1},{33,17},{49,33},{1,49},{18,2}... | collective-permute-start | bytes 1179656 | tf_op jit(solution)/shard_map/ppermute | solution.py:32
  49.5 15.9 %collective-permute-start.4 = (f32[48,1024]{1,0:T(8,128)S(1)}, f32[48,1024]{1,0:T(8,128)S(1)}, u32[]{:S(2)}, u32[]{:S(2)}) collective-permute-start(f32[48,1024]{1,0:T(8,128)S(1)} %get-tuple-element.11), channel_id=1, source_target_pairs={{0,2},{2,4},{4,6},{6,0},{1,3},{3,5},{5,7},{7,1},{8,10},{10,12},{12... | collective-permute-start | bytes 589832 | tf_op jit(solution)/shard_map/ppermute | solution.py:44
  55.0 12.3 %collective-permute-start.7 = (f32[48,1024]{1,0:T(8,128)S(1)}, f32[48,1024]{1,0:T(8,128)S(1)}, u32[]{:S(2)}, u32[]{:S(2)}) collective-permute-start(f32[48,1024]{1,0:T(8,128)S(1)} %get-tuple-element.12), channel_id=1, source_target_pairs={{0,6},{2,0},{4,2},{6,4},{1,7},{3,1},{5,3},{7,5},{8,14},{10,8},{12,... | collective-permute-start | bytes 589832 | tf_op jit(solution)/shard_map/ppermute | solution.py:45
  61.0 11.9 %collective-permute-start.3 = (f32[96,1024]{1,0:T(8,128)S(1)}, f32[96,1024]{1,0:T(8,128)S(1)}, u32[]{:S(2)}, u32[]{:S(2)}) collective-permute-start(f32[96,1024]{1,0:T(8,128)S(1)} %bitcast.27), channel_id=1, source_target_pairs={{32,0},{48,16},{0,32},{16,48},{33,1},{49,17},{1,33},{17,49},{34,2}... | collective-permute-start | bytes 1179656 | tf_op jit(solution)/shard_map/ppermute | solution.py:32
  65.4 11.4 %collective-permute-start.5 = (f32[96,1024]{1,0:T(8,128)S(1)}, f32[96,1024]{1,0:T(8,128)S(1)}, u32[]{:S(2)}, u32[]{:S(2)}) collective-permute-start(f32[96,1024]{1,0:T(8,128)S(1)} %pad_maximum_fusion.1), channel_id=1, source_target_pairs={{0,2},{2,4},{4,6},{6,0},{1,3},{3,5},{5,7},{7,1},{8,10},{10,12},{12... | collective-permute-start | bytes 1179656 | tf_op jit(solution)/shard_map/ppermute | solution.py:48
  67.4 10.3 %collective-permute-start.8 = (f32[96,1024]{1,0:T(8,128)S(1)}, f32[96,1024]{1,0:T(8,128)S(1)}, u32[]{:S(2)}, u32[]{:S(2)}) collective-permute-start(f32[96,1024]{1,0:T(8,128)S(1)} %pad_maximum_fusion.2), channel_id=1, source_target_pairs={{0,6},{2,0},{4,2},{6,4},{1,7},{3,1},{5,3},{7,5},{8,14},{10,8},{12,... | collective-permute-start | bytes 1179656 | tf_op jit(solution)/shard_map/ppermute | solution.py:51

commit v4 on v3

--- a/solution.py
+++ b/solution.py
@@ -1,3 +1,5 @@
+import itertools
+
 import jax
 import jax.numpy as jnp
 from jax import lax
@@ -28,31 +30,33 @@
     near = jnp.where(lax.axis_index("c") == 0, near, near[:, ::-1])
     near = near.transpose(0, 2, 1, 3).reshape(Y * ZL * share, C * depth)
 
-    def fetch(source, step):
-        return lax.ppermute(source, "x", [((x + step) % X, x) for x in range(X)])
+    def paired(block, pairing):
+        target = lambda d, c: (d + (1 if (d + c + pairing) % 2 == 0 else -1)) % ZH
+        pairs = [(d * C + c, target(d, c) * C + c) for d in range(ZH) for c in range(C)]
+        return lax.ppermute(block, ("zh", "c"), pairs)
+
+    def fetch(source, pairing):
+        pairs = []
+        for x, d, c in itertools.product(range(X), range(ZH), range(C)):
+            step = -1 if (d + c + pairing) % 2 == 0 else 1
+            pairs.append((((x + step) % X * ZH + d) * C + c, (x * ZH + d) * C + c))
+        return lax.ppermute(source, ("x", "zh", "c"), pairs)
 
     def term(block):
         return lax.dot_general(
             block, held, (((1,), (1,)), ((), ())), precision=lax.Precision.HIGH
         )
 
-    up = [(d, (d + 1) % ZH) for d in range(ZH)]
-    down = [(d, (d - 1) % ZH) for d in range(ZH)]
-    next_one, last_one = fetch(near, -1), fetch(near, 1)
-    opposite = term(near)
-    cut = opposite.shape[0] // 2
-    from_below = lax.ppermute(opposite[:cut], "zh", up)
-    from_above = lax.ppermute(opposite[cut:], "zh", down)
-    above, below = term(next_one), term(last_one)
-    near, above = lax.optimization_barrier((near, above))
-    arrived_up = lax.ppermute(
-        jnp.concatenate([above[:cut] + from_below, above[cut:]]), "zh", up
-    )
-    arrived_down = lax.ppermute(
-        jnp.concatenate([below[:cut], below[cut:] + from_above]), "zh", down
-    )
-    mine = lax.optimization_barrier(term(fetch(near, 2)))
-    summed = mine + arrived_up + arrived_down
+    block_a, block_b = fetch(near, 0), fetch(near, 1)
+    passed = paired(term(near), 0)
+    term_a = term(block_a)
+    from_a = paired(term_a, 0)
+    near, term_a = lax.optimization_barrier((near, term_a))
+    from_a, sent_b = lax.optimization_barrier((from_a, term(block_b) + passed))
+    from_b = paired(sent_b, 1)
+    block = lax.ppermute(near, "x", [((x + 2) % X, x) for x in range(X)])
+    mine = lax.optimization_barrier(term(block))
+    summed = mine + from_a + from_b
     tile = sum(
         lax.dot_general(
             summed[:, p * rows : p * rows + half],

time: 126 us -> 121 us (0.960)
  blocking collectives: 46 us -> 32.3 us
  waiting for transfers between devices: 22.1 us -> 32.5 us
  starting transfers between devices: 43.2 us -> 41.4 us
    all_to_all x1, blocking collectives: 30.1 us -> 15.9 us  [body(): lax.all_to_all(tile.reshape(Y * X, ZL * m, half), ('y', 'x'), 0, 0, tiled...]
    ppermute x7 -> x6, waiting for transfers between devices: 3.84 us -> 14.3 us  [the longest x3 14.3 us: paired(): return lax.ppermute(block, ('zh', 'c'), pairs)]
    ppermute x7 -> x6, starting transfers between devices: 27.5 us -> 25.7 us  [the longest x3 16.2 us: paired(): return lax.ppermute(block, ('zh', 'c'), pairs)]
  transfers between devices with their start and end apart: 10 -> 9, of which waited for: 5 -> 4; matrix products, arithmetic and copies ran while one was open for 10% -> 10% of each run, Pallas kernels for 0% -> 0%
where the time goes in v4:
time: 121 us; the launch traced here: 120 us
  starting transfers between devices  41.4 us (34%)
  waiting for transfers between devices  32.5 us (27%)
  blocking collectives  32.3 us (27%)
  matrix products  9.61 us (8%)
  other arithmetic  2.21 us (2%)
  local copies, waits for them, and re-layouts  2.04 us (2%)
    all_to_all x1, blocking collectives, body(): lax.all_to_all(tile.reshape(ZL * ZH * C, m * n), ('zl', 'zh', 'c'), 0, 0,...  16.4 us
    ppermute x3, starting transfers between devices, paired(): return lax.ppermute(block, ('zh', 'c'), pairs)  16.2 us
    all_to_all x1, blocking collectives, body(): lax.all_to_all(tile.reshape(Y * X, ZL * m, half), ('y', 'x'), 0, 0, tiled...  15.9 us
    ppermute x3, waiting for transfers between devices, paired(): return lax.ppermute(block, ('zh', 'c'), pairs)  14.3 us
    all_to_all x1, waiting for transfers between devices, body(): lax.all_to_all(sent.reshape(Y * ZL * C, -1, LANES), ('y', 'zl', 'c'), 0,...  13.8 us
    ppermute x1, starting transfers between devices, body(): swapped = lax.ppermute(integrals, 'c', [(0, 1), (1, 0)])  8.91 us
    dot_general x4, matrix products, term(): lax.dot_general(block, held, (((1,), (1,)), ((), ())), precision=lax.Prec...  8.78 us
    ppermute x2, starting transfers between devices, fetch(): return lax.ppermute(source, ('x', 'zh', 'c'), pairs)  6.49 us
  transfers between devices with their start and end apart: 9, of which 4 were waited for; matrix products, arithmetic and copies ran while one was open for 10% of the time, Pallas kernels for 0%

profile of v4, /device:TPU:1, one launch (start us, length us, event | category | flops | bytes accessed | tf_op | source)
XLA Modules:
  0.0 120.2 jit_solution(1867387240211976461)
XLA Ops:
  0.0 0.0 copy-start
  0.0 8.9 %collective-permute-start.2 = (f32[2,512,512]{2,1,0:T(8,128)}, f32[2,512,512]{2,1,0:T(8,128)}, u32[]{:S(2)}, u32[]{:S(2)}) collective-permute-start(f32[2,512,512]{2,1,0:T(8,128)} %param.2), channel_id=1, source_target_pairs={{0,1},{1,0},{2,3},{3,2},{4,5},{5,4},{6,7},{7,6},{8,9},{9,8},{10,11... | collective-permute-start | bytes 6291464 | tf_op jit(solution)/shard_map/ppermute | solution.py:18
  8.9 1.9 %collective-permute-start = (f32[12,512]{1,0:T(8,128)}, f32[12,512]{1,0:T(8,128)S(1)}, u32[]{:S(2)}, u32[]{:S(2)}) collective-permute-start(f32[12,512]{1,0:T(8,128)} %bitcast.31), channel_id=1, source_target_pairs={{32,0},{50,2},{4,4},{22,6},{48,16},{2,18},{20,20},{38,22},{0,32},{... | collective-permute-start | bytes 73736 | tf_op jit(solution)/shard_map/ppermute | solution.py:22
  10.8 4.4 %collective-permute-done = f32[12,512]{1,0:T(8,128)S(1)} collective-permute-done((f32[12,512]{1,0:T(8,128)}, f32[12,512]{1,0:T(8,128)S(1)}, u32[]{:S(2)}, u32[]{:S(2)}) %collective-permute-start) | collective-permute-done | bytes 24608 | tf_op jit(solution)/shard_map/ppermute | solution.py:22
  15.3 0.8 broadcast_in_dim.3
  16.1 4.9 %all-to-all-start = ((f32[32,24,128]{2,1,0:T(8,128)}), f32[32,24,128]{2,1,0:T(8,128)S(1)}, u32[]{:S(2)}, u32[]{:S(2)}) async-start(f32[32,24,128]{2,1,0:T(8,128)} %bitcast.1), calls=%async_computation | async-start | bytes 786432 | tf_op jit(solution)/shard_map/all_to_all | solution.py:27
  20.9 13.8 %all-to-all-done = f32[32,24,128]{2,1,0:T(8,128)S(1)} async-done(((f32[32,24,128]{2,1,0:T(8,128)}), f32[32,24,128]{2,1,0:T(8,128)S(1)}, u32[]{:S(2)}, u32[]{:S(2)}) %all-to-all-start) | async-done | bytes 393248 | tf_op jit(solution)/shard_map/all_to_all | solution.py:27
  34.7 0.1 reshape.30
  34.8 0.3 copy.6
  35.1 0.1 copy.9
  35.2 3.1 %collective-permute-start.5 = (f32[96,1024]{1,0:T(8,128)S(1)}, f32[96,1024]{1,0:T(8,128)S(1)}, u32[]{:S(2)}, u32[]{:S(2)}) collective-permute-start(f32[96,1024]{1,0:T(8,128)S(1)} %bitcast.24), channel_id=1, source_target_pairs={{16,0},{49,1},{50,2},{19,3},{20,4},{53,5},{54,6},{23,7},{32,16},{1... | collective-permute-start | bytes 1179656 | tf_op jit(solution)/shard_map/ppermute | solution.py:43
  38.3 3.4 %collective-permute-start.1 = (f32[96,1024]{1,0:T(8,128)S(1)}, f32[96,1024]{1,0:T(8,128)S(1)}, u32[]{:S(2)}, u32[]{:S(2)}) collective-permute-start(f32[96,1024]{1,0:T(8,128)S(1)} %bitcast.25), channel_id=1, source_target_pairs={{48,0},{17,1},{18,2},{51,3},{52,4},{21,5},{22,6},{55,7},{0,16},{33... | collective-permute-start | bytes 1179656 | tf_op jit(solution)/shard_map/ppermute | solution.py:43
  41.7 0.0 collective-permute-done.2
  41.7 0.0 copy-done
  41.7 2.0 %pad_maximum_fusion = f32[2,512,1024]{2,1,0:T(8,128)S(1)} fusion(f32[2,512,512]{2,1,0:T(8,128)} %collective-permute-done.2, f32[2,512,512]{2,1,0:T(8,128)S(1)} %copy-done), kind=kLoop, calls=%fused_computation | loop fusion | flops 1048576 | bytes 8388608 | tf_op jit(solution)/shard_map/concatenate | solution.py:19
  43.8 2.2 %fusion.9 = f32[96,1024]{1,0:T(8,128)S(1)} fusion(f32[96,1024]{1,0:T(8,128)S(1)} %bitcast.26, f32[1024,1024]{1,0:T(8,128)S(1)} %bitcast.20), kind=kOutput, calls=%fused_computation.14 | convolution fusion | flops 603979776 | bytes 4980736 | tf_op jit(solution)/shard_map/dot_general | solution.py:46
  46.0 9.3 %collective-permute-start.6 = (f32[96,1024]{1,0:T(8,128)S(1)}, f32[96,1024]{1,0:T(8,128)S(1)}, u32[]{:S(2)}, u32[]{:S(2)}) collective-permute-start(f32[96,1024]{1,0:T(8,128)S(1)} %fusion.9), channel_id=1, source_target_pairs={{0,2},{1,7},{2,0},{3,5},{4,6},{5,3},{6,4},{7,1},{8,10},{9,15},{10,... | collective-permute-start | bytes 1179656 | tf_op jit(solution)/shard_map/ppermute | solution.py:36
  55.3 0.0 collective-permute-done.1
  55.3 2.2 %fusion.7 = f32[96,1024]{1,0:T(8,128)S(1)} fusion(f32[96,1024]{1,0:T(8,128)S(1)} %collective-permute-done.1, f32[1024,1024]{1,0:T(8,128)S(1)} %bitcast.21), kind=kOutput, calls=%fused_computation.12 | convolution fusion | flops 603979776 | bytes 4980736 | tf_op jit(solution)/shard_map/dot_general | solution.py:46
  57.5 5.0 %collective-permute-start.4 = (f32[96,1024]{1,0:T(8,128)S(1)}, f32[96,1024]{1,0:T(8,128)S(1)}, u32[]{:S(2)}, u32[]{:S(2)}) collective-permute-start(f32[96,1024]{1,0:T(8,128)S(1)} %fusion.7), channel_id=1, source_target_pairs={{0,2},{1,7},{2,0},{3,5},{4,6},{5,3},{6,4},{7,1},{8,10},{9,15},{10,... | collective-permute-start | bytes 1179656 | tf_op jit(solution)/shard_map/ppermute | solution.py:36
  62.5 3.0 %collective-permute-start.3 = (f32[96,1024]{1,0:T(8,128)S(1)}, f32[96,1024]{1,0:T(8,128)S(1)}, u32[]{:S(2)}, u32[]{:S(2)}) collective-permute-start(f32[96,1024]{1,0:T(8,128)S(1)} %bitcast.27), channel_id=1, source_target_pairs={{32,0},{48,16},{0,32},{16,48},{33,1},{49,17},{1,33},{17,49},{34,2}... | collective-permute-start | bytes 1179656 | tf_op jit(solution)/shard_map/ppermute | solution.py:57
  65.5 0.0 collective-permute-done.5
  65.5 0.0 collective-permute-done.6
  65.5 2.2 %convolution_add_fusion = f32[96,1024]{1,0:T(8,128)S(1)} fusion(f32[96,1024]{1,0:T(8,128)S(1)} %collective-permute-done.6, f32[96,1024]{1,0:T(8,128)S(1)} %collective-permute-done.5, f32[1024,1024]{1,0:T(8,128)S(1)} %bitcast.22), kind=kOutput, calls=%fused_computation.1 | convolution fusion | flops 604078080 | bytes 5373952 | tf_op jit(solution)/shard_map/dot_general | solution.py:46
  67.7 4.7 %collective-permute-done.4 = f32[96,1024]{1,0:T(8,128)S(1)} collective-permute-done((f32[96,1024]{1,0:T(8,128)S(1)}, f32[96,1024]{1,0:T(8,128)S(1)}, u32[]{:S(2)}, u32[]{:S(2)}) %collective-permute-start.4) | collective-permute-done | bytes 393248 | tf_op jit(solution)/shard_map/ppermute | solution.py:36
  72.4 1.9 %collective-permute-start.7 = (f32[96,1024]{1,0:T(8,128)S(1)}, f32[96,1024]{1,0:T(8,128)S(1)}, u32[]{:S(2)}, u32[]{:S(2)}) collective-permute-start(f32[96,1024]{1,0:T(8,128)S(1)} %convolution_add_fusion), channel_id=1, source_target_pairs={{0,6},{1,3},{2,4},{3,1},{4,2},{5,7},{6,0},{7,5},{8,14},{9,11},{10,... | collective-permute-start | bytes 1179656 | tf_op jit(solution)/shard_map/ppermute | solution.py:36
  74.3 0.0 collective-permute-done.3
  74.3 2.2 %fusion.8 = f32[96,1024]{1,0:T(8,128)S(1)} fusion(f32[96,1024]{1,0:T(8,128)S(1)} %collective-permute-done.3, f32[1024,1024]{1,0:T(8,128)S(1)} %bitcast.23), kind=kOutput, calls=%fused_computation.13 | convolution fusion | flops 603979776 | bytes 4980736 | tf_op jit(solution)/shard_map/dot_general | solution.py:46
  76.5 9.6 %collective-permute-done.7 = f32[96,1024]{1,0:T(8,128)S(1)} collective-permute-done((f32[96,1024]{1,0:T(8,128)S(1)}, f32[96,1024]{1,0:T(8,128)S(1)}, u32[]{:S(2)}, u32[]{:S(2)}) %collective-permute-start.7) | collective-permute-done | bytes 393248 | tf_op jit(solution)/shard_map/ppermute | solution.py:36
  86.1 0.1 add_add_fusion
  86.2 0.4 fusion.2
  86.6 0.4 fusion
  87.0 15.9 %all_to_all.19 = f32[32,8,256]{2,1,0:T(8,128)S(1)} all-to-all(f32[32,8,256]{2,1,0:T(8,128)S(1)} %fusion), channel_id=1, replica_groups=mesh['y'=8,'x'=4,'zl'=2,'zh'=4,'c'=2] {'y','x'}, dimensions={0} | all-to-all | bytes 524288 | tf_op jit(solution)/shard_map/all_to_all | solution.py:71
  102.9 0.1 reshape.34
  103.0 0.1 all_to_all.14
  103.1 16.4 %all_to_all.20 = f32[16,1,128]{2,1,0:T(1,128)S(1)} all-to-all(f32[16,1,128]{2,1,0:T(1,128)S(1)} %bitcast.30), channel_id=1, replica_groups=mesh['y'=8,'x'=4,'zl'=2,'zh'=4,'c'=2] {'zl','zh','c'}, dimensions={0} | all-to-all | bytes 16384 | tf_op jit(solution)/shard_map/all_to_all | solution.py:73
  119.6 0.7 reshape.35
  (5 shorter events, 0.1 us)
Async XLA Ops:
  0.0 41.7 %copy-start = (f32[2,512,512]{2,1,0:T(8,128)S(1)}, f32[2,512,512]{2,1,0:T(8,128)}, u32[]{:S(2)}) copy-start(f32[2,512,512]{2,1,0:T(8,128)} %param.2) | copy-start | bytes 6291460
  0.0 41.7 %collective-permute-start.2 = (f32[2,512,512]{2,1,0:T(8,128)}, f32[2,512,512]{2,1,0:T(8,128)}, u32[]{:S(2)}, u32[]{:S(2)}) collective-permute-start(f32[2,512,512]{2,1,0:T(8,128)} %param.2), channel_id=1, source_target_pairs={{0,1},{1,0},{2,3},{3,2},{4,5},{5,4},{6,7},{7,6},{8,9},{9,8},{10,11... | collective-permute-start | bytes 6291464 | tf_op jit(solution)/shard_map/ppermute | solution.py:18
  8.9 6.4 %collective-permute-start = (f32[12,512]{1,0:T(8,128)}, f32[12,512]{1,0:T(8,128)S(1)}, u32[]{:S(2)}, u32[]{:S(2)}) collective-permute-start(f32[12,512]{1,0:T(8,128)} %bitcast.31), channel_id=1, source_target_pairs={{32,0},{50,2},{4,4},{22,6},{48,16},{2,18},{20,20},{38,22},{0,32},{... | collective-permute-start | bytes 73736 | tf_op jit(solution)/shard_map/ppermute | solution.py:22
  16.1 18.6 %all-to-all-start = ((f32[32,24,128]{2,1,0:T(8,128)}), f32[32,24,128]{2,1,0:T(8,128)S(1)}, u32[]{:S(2)}, u32[]{:S(2)}) async-start(f32[32,24,128]{2,1,0:T(8,128)} %bitcast.1), calls=%async_computation | async-start | bytes 786432 | tf_op jit(solution)/shard_map/all_to_all | solution.py:27
  35.2 30.3 %collective-permute-start.5 = (f32[96,1024]{1,0:T(8,128)S(1)}, f32[96,1024]{1,0:T(8,128)S(1)}, u32[]{:S(2)}, u32[]{:S(2)}) collective-permute-start(f32[96,1024]{1,0:T(8,128)S(1)} %bitcast.24), channel_id=1, source_target_pairs={{16,0},{49,1},{50,2},{19,3},{20,4},{53,5},{54,6},{23,7},{32,16},{1... | collective-permute-start | bytes 1179656 | tf_op jit(solution)/shard_map/ppermute | solution.py:43
  38.3 16.9 %collective-permute-start.1 = (f32[96,1024]{1,0:T(8,128)S(1)}, f32[96,1024]{1,0:T(8,128)S(1)}, u32[]{:S(2)}, u32[]{:S(2)}) collective-permute-start(f32[96,1024]{1,0:T(8,128)S(1)} %bitcast.25), channel_id=1, source_target_pairs={{48,0},{17,1},{18,2},{51,3},{52,4},{21,5},{22,6},{55,7},{0,16},{33... | collective-permute-start | bytes 1179656 | tf_op jit(solution)/shard_map/ppermute | solution.py:43
  46.0 19.5 %collective-permute-start.6 = (f32[96,1024]{1,0:T(8,128)S(1)}, f32[96,1024]{1,0:T(8,128)S(1)}, u32[]{:S(2)}, u32[]{:S(2)}) collective-permute-start(f32[96,1024]{1,0:T(8,128)S(1)} %fusion.9), channel_id=1, source_target_pairs={{0,2},{1,7},{2,0},{3,5},{4,6},{5,3},{6,4},{7,1},{8,10},{9,15},{10,... | collective-permute-start | bytes 1179656 | tf_op jit(solution)/shard_map/ppermute | solution.py:36
  57.5 14.9 %collective-permute-start.4 = (f32[96,1024]{1,0:T(8,128)S(1)}, f32[96,1024]{1,0:T(8,128)S(1)}, u32[]{:S(2)}, u32[]{:S(2)}) collective-permute-start(f32[96,1024]{1,0:T(8,128)S(1)} %fusion.7), channel_id=1, source_target_pairs={{0,2},{1,7},{2,0},{3,5},{4,6},{5,3},{6,4},{7,1},{8,10},{9,15},{10,... | collective-permute-start | bytes 1179656 | tf_op jit(solution)/shard_map/ppermute | solution.py:36
  62.5 11.8 %collective-permute-start.3 = (f32[96,1024]{1,0:T(8,128)S(1)}, f32[96,1024]{1,0:T(8,128)S(1)}, u32[]{:S(2)}, u32[]{:S(2)}) collective-permute-start(f32[96,1024]{1,0:T(8,128)S(1)} %bitcast.27), channel_id=1, source_target_pairs={{32,0},{48,16},{0,32},{16,48},{33,1},{49,17},{1,33},{17,49},{34,2}... | collective-permute-start | bytes 1179656 | tf_op jit(solution)/shard_map/ppermute | solution.py:57
  72.4 13.7 %collective-permute-start.7 = (f32[96,1024]{1,0:T(8,128)S(1)}, f32[96,1024]{1,0:T(8,128)S(1)}, u32[]{:S(2)}, u32[]{:S(2)}) collective-permute-start(f32[96,1024]{1,0:T(8,128)S(1)} %convolution_add_fusion), channel_id=1, source_target_pairs={{0,6},{1,3},{2,4},{3,1},{4,2},{5,7},{6,0},{7,5},{8,14},{9,11},{10,... | collective-permute-start | bytes 1179656 | tf_op jit(solution)/shard_map/ppermute | solution.py:36

commit v5 on v4

--- a/solution.py
+++ b/solution.py
@@ -50,13 +50,14 @@
     block_a, block_b = fetch(near, 0), fetch(near, 1)
     passed = paired(term(near), 0)
     term_a = term(block_a)
-    from_a = paired(term_a, 0)
+    cut = term_a.shape[0] // 2
+    from_a, later_a = paired(term_a[:cut], 0), paired(term_a[cut:], 0)
     near, term_a = lax.optimization_barrier((near, term_a))
     from_a, sent_b = lax.optimization_barrier((from_a, term(block_b) + passed))
     from_b = paired(sent_b, 1)
     block = lax.ppermute(near, "x", [((x + 2) % X, x) for x in range(X)])
     mine = lax.optimization_barrier(term(block))
-    summed = mine + from_a + from_b
+    summed = mine + jnp.concatenate([from_a, later_a]) + from_b
     tile = sum(
         lax.dot_general(
             summed[:, p * rows : p * rows + half],

time: 121 us -> 121 us (level)
  starting transfers between devices: 41.4 us -> 47.9 us
  waiting for transfers between devices: 32.5 us -> 27.6 us
    ppermute x3 -> x4, starting transfers between devices: 16.2 us -> 22.7 us  [paired(): return lax.ppermute(block, ('zh', 'c'), pairs)]
    ppermute x3 -> x4, waiting for transfers between devices: 14.3 us -> 9.38 us  [paired(): return lax.ppermute(block, ('zh', 'c'), pairs)]
  transfers between devices with their start and end apart: 9 -> 10, of which waited for: 4 -> 4; matrix products, arithmetic and copies ran while one was open for 10% -> 10% of each run, Pallas kernels for 0% -> 0%
where the time goes in v5:
time: 121 us
  starting transfers between devices  47.9 us (40%)
  blocking collectives  31.3 us (26%)
  waiting for transfers between devices  27.6 us (23%)
  matrix products  9.61 us (8%)
  other arithmetic  2.21 us (2%)
  local copies, waits for them, and re-layouts  2.08 us (2%)
    ppermute x4, starting transfers between devices, paired(): return lax.ppermute(block, ('zh', 'c'), pairs)  22.7 us
    all_to_all x1, blocking collectives, body(): lax.all_to_all(tile.reshape(ZL * ZH * C, m * n), ('zl', 'zh', 'c'), 0, 0,...  15.9 us
    all_to_all x1, blocking collectives, body(): lax.all_to_all(tile.reshape(Y * X, ZL * m, half), ('y', 'x'), 0, 0, tiled...  15.4 us
    all_to_all x1, waiting for transfers between devices, body(): lax.all_to_all(sent.reshape(Y * ZL * C, -1, LANES), ('y', 'zl', 'c'), 0,...  13.8 us
    ppermute x4, waiting for transfers between devices, paired(): return lax.ppermute(block, ('zh', 'c'), pairs)  9.38 us
    ppermute x1, starting transfers between devices, body(): swapped = lax.ppermute(integrals, 'c', [(0, 1), (1, 0)])  8.91 us
    dot_general x4, matrix products, term(): lax.dot_general(block, held, (((1,), (1,)), ((), ())), precision=lax.Prec...  8.78 us
    ppermute x2, starting transfers between devices, fetch(): return lax.ppermute(source, ('x', 'zh', 'c'), pairs)  6.49 us
  transfers between devices with their start and end apart: 10, of which 4 were waited for; matrix products, arithmetic and copies ran while one was open for 10% of the time, Pallas kernels for 0%

profile of v5, /device:TPU:1, one launch (start us, length us, event | category | flops | bytes accessed | tf_op | source)
XLA Modules:
  0.0 120.9 jit_solution(12059213710164190789)
XLA Ops:
  0.0 0.0 copy-start
  0.0 8.9 %collective-permute-start.2 = (f32[2,512,512]{2,1,0:T(8,128)}, f32[2,512,512]{2,1,0:T(8,128)}, u32[]{:S(2)}, u32[]{:S(2)}) collective-permute-start(f32[2,512,512]{2,1,0:T(8,128)} %param.2), channel_id=1, source_target_pairs={{0,1},{1,0},{2,3},{3,2},{4,5},{5,4},{6,7},{7,6},{8,9},{9,8},{10,11... | collective-permute-start | bytes 6291464 | tf_op jit(solution)/shard_map/ppermute | solution.py:18
  8.9 1.9 %collective-permute-start = (f32[12,512]{1,0:T(8,128)}, f32[12,512]{1,0:T(8,128)S(1)}, u32[]{:S(2)}, u32[]{:S(2)}) collective-permute-start(f32[12,512]{1,0:T(8,128)} %bitcast.31), channel_id=1, source_target_pairs={{32,0},{50,2},{4,4},{22,6},{48,16},{2,18},{20,20},{38,22},{0,32},{... | collective-permute-start | bytes 73736 | tf_op jit(solution)/shard_map/ppermute | solution.py:22
  10.8 4.4 %collective-permute-done = f32[12,512]{1,0:T(8,128)S(1)} collective-permute-done((f32[12,512]{1,0:T(8,128)}, f32[12,512]{1,0:T(8,128)S(1)}, u32[]{:S(2)}, u32[]{:S(2)}) %collective-permute-start) | collective-permute-done | bytes 24608 | tf_op jit(solution)/shard_map/ppermute | solution.py:22
  15.3 0.8 broadcast_in_dim.3
  16.1 4.9 %all-to-all-start = ((f32[32,24,128]{2,1,0:T(8,128)}), f32[32,24,128]{2,1,0:T(8,128)S(1)}, u32[]{:S(2)}, u32[]{:S(2)}) async-start(f32[32,24,128]{2,1,0:T(8,128)} %bitcast.1), calls=%async_computation | async-start | bytes 786432 | tf_op jit(solution)/shard_map/all_to_all | solution.py:27
  20.9 13.8 %all-to-all-done = f32[32,24,128]{2,1,0:T(8,128)S(1)} async-done(((f32[32,24,128]{2,1,0:T(8,128)}), f32[32,24,128]{2,1,0:T(8,128)S(1)}, u32[]{:S(2)}, u32[]{:S(2)}) %all-to-all-start) | async-done | bytes 393248 | tf_op jit(solution)/shard_map/all_to_all | solution.py:27
  34.7 0.1 reshape.30
  34.8 0.3 copy.6
  35.1 0.1 copy.9
  35.2 3.1 %collective-permute-start.5 = (f32[96,1024]{1,0:T(8,128)S(1)}, f32[96,1024]{1,0:T(8,128)S(1)}, u32[]{:S(2)}, u32[]{:S(2)}) collective-permute-start(f32[96,1024]{1,0:T(8,128)S(1)} %bitcast.24), channel_id=1, source_target_pairs={{16,0},{49,1},{50,2},{19,3},{20,4},{53,5},{54,6},{23,7},{32,16},{1... | collective-permute-start | bytes 1179656 | tf_op jit(solution)/shard_map/ppermute | solution.py:43
  38.3 3.4 %collective-permute-start.1 = (f32[96,1024]{1,0:T(8,128)S(1)}, f32[96,1024]{1,0:T(8,128)S(1)}, u32[]{:S(2)}, u32[]{:S(2)}) collective-permute-start(f32[96,1024]{1,0:T(8,128)S(1)} %bitcast.25), channel_id=1, source_target_pairs={{48,0},{17,1},{18,2},{51,3},{52,4},{21,5},{22,6},{55,7},{0,16},{33... | collective-permute-start | bytes 1179656 | tf_op jit(solution)/shard_map/ppermute | solution.py:43
  41.7 0.0 collective-permute-done.2
  41.7 0.0 copy-done
  41.7 2.0 %pad_maximum_fusion = f32[2,512,1024]{2,1,0:T(8,128)S(1)} fusion(f32[2,512,512]{2,1,0:T(8,128)} %collective-permute-done.2, f32[2,512,512]{2,1,0:T(8,128)S(1)} %copy-done), kind=kLoop, calls=%fused_computation | loop fusion | flops 1048576 | bytes 8388608 | tf_op jit(solution)/shard_map/concatenate | solution.py:19
  43.8 2.2 %fusion.11 = f32[96,1024]{1,0:T(8,128)S(1)} fusion(f32[96,1024]{1,0:T(8,128)S(1)} %bitcast.26, f32[1024,1024]{1,0:T(8,128)S(1)} %bitcast.20), kind=kOutput, calls=%fused_computation.16 | convolution fusion | flops 603979776 | bytes 4980736 | tf_op jit(solution)/shard_map/dot_general | solution.py:46
  46.0 9.3 %collective-permute-start.6 = (f32[96,1024]{1,0:T(8,128)S(1)}, f32[96,1024]{1,0:T(8,128)S(1)}, u32[]{:S(2)}, u32[]{:S(2)}) collective-permute-start(f32[96,1024]{1,0:T(8,128)S(1)} %fusion.11), channel_id=1, source_target_pairs={{0,2},{1,7},{2,0},{3,5},{4,6},{5,3},{6,4},{7,1},{8,10},{9,15},{10,... | collective-permute-start | bytes 1179656 | tf_op jit(solution)/shard_map/ppermute | solution.py:36
  55.3 0.0 collective-permute-done.1
  55.3 2.2 %fusion.9 = f32[96,1024]{1,0:T(8,128)S(1)} fusion(f32[96,1024]{1,0:T(8,128)S(1)} %collective-permute-done.1, f32[1024,1024]{1,0:T(8,128)S(1)} %bitcast.21), kind=kOutput, calls=%fused_computation.14 | convolution fusion | flops 603979776 | bytes 4980736 | tf_op jit(solution)/shard_map/dot_general | solution.py:46
  57.5 5.0 %collective-permute-start.4 = (f32[48,1024]{1,0:T(8,128)S(1)}, f32[48,1024]{1,0:T(8,128)S(1)}, u32[]{:S(2)}, u32[]{:S(2)}) collective-permute-start(f32[48,1024]{1,0:T(8,128)S(1)} %get-tuple-element.12), channel_id=1, source_target_pairs={{0,2},{1,7},{2,0},{3,5},{4,6},{5,3},{6,4},{7,1},{8,10},{9,15},{10,... | collective-permute-start | bytes 589832 | tf_op jit(solution)/shard_map/ppermute | solution.py:36
  62.5 3.0 %collective-permute-start.3 = (f32[96,1024]{1,0:T(8,128)S(1)}, f32[96,1024]{1,0:T(8,128)S(1)}, u32[]{:S(2)}, u32[]{:S(2)}) collective-permute-start(f32[96,1024]{1,0:T(8,128)S(1)} %bitcast.27), channel_id=1, source_target_pairs={{32,0},{48,16},{0,32},{16,48},{33,1},{49,17},{1,33},{17,49},{34,2}... | collective-permute-start | bytes 1179656 | tf_op jit(solution)/shard_map/ppermute | solution.py:58
  65.5 0.0 collective-permute-done.5
  65.6 0.0 collective-permute-done.6
  65.6 2.2 %convolution_add_fusion = f32[96,1024]{1,0:T(8,128)S(1)} fusion(f32[96,1024]{1,0:T(8,128)S(1)} %collective-permute-done.6, f32[96,1024]{1,0:T(8,128)S(1)} %collective-permute-done.5, f32[1024,1024]{1,0:T(8,128)S(1)} %bitcast.22), kind=kOutput, calls=%fused_computation.1 | convolution fusion | flops 604078080 | bytes 5373952 | tf_op jit(solution)/shard_map/dot_general | solution.py:46
  67.8 0.7 collective-permute-done.4
  68.5 1.9 %collective-permute-start.8 = (f32[96,1024]{1,0:T(8,128)S(1)}, f32[96,1024]{1,0:T(8,128)S(1)}, u32[]{:S(2)}, u32[]{:S(2)}) collective-permute-start(f32[96,1024]{1,0:T(8,128)S(1)} %convolution_add_fusion), channel_id=1, source_target_pairs={{0,6},{1,3},{2,4},{3,1},{4,2},{5,7},{6,0},{7,5},{8,14},{9,11},{10,... | collective-permute-start | bytes 1179656 | tf_op jit(solution)/shard_map/ppermute | solution.py:36
  70.4 6.5 %collective-permute-start.7 = (f32[48,1024]{1,0:T(8,128)S(1)}, f32[48,1024]{1,0:T(8,128)S(1)}, u32[]{:S(2)}, u32[]{:S(2)}) collective-permute-start(f32[48,1024]{1,0:T(8,128)S(1)} %get-tuple-element.11), channel_id=1, source_target_pairs={{0,2},{1,7},{2,0},{3,5},{4,6},{5,3},{6,4},{7,1},{8,10},{9,15},{10,... | collective-permute-start | bytes 589832 | tf_op jit(solution)/shard_map/ppermute | solution.py:36
  76.9 0.0 collective-permute-done.3
  76.9 2.2 %fusion.10 = f32[96,1024]{1,0:T(8,128)S(1)} fusion(f32[96,1024]{1,0:T(8,128)S(1)} %collective-permute-done.3, f32[1024,1024]{1,0:T(8,128)S(1)} %bitcast.23), kind=kOutput, calls=%fused_computation.15 | convolution fusion | flops 603979776 | bytes 4980736 | tf_op jit(solution)/shard_map/dot_general | solution.py:46
  79.1 8.7 %collective-permute-done.7 = f32[48,1024]{1,0:T(8,128)S(1)} collective-permute-done((f32[48,1024]{1,0:T(8,128)S(1)}, f32[48,1024]{1,0:T(8,128)S(1)}, u32[]{:S(2)}, u32[]{:S(2)}) %collective-permute-start.7) | collective-permute-done | bytes 196640 | tf_op jit(solution)/shard_map/ppermute | solution.py:36
  87.8 0.0 collective-permute-done.8
  87.8 0.1 fusion.2
  87.9 0.4 fusion.3
  88.3 0.4 fusion
  88.7 15.4 %all_to_all.19 = f32[32,8,256]{2,1,0:T(8,128)S(1)} all-to-all(f32[32,8,256]{2,1,0:T(8,128)S(1)} %fusion), channel_id=1, replica_groups=mesh['y'=8,'x'=4,'zl'=2,'zh'=4,'c'=2] {'y','x'}, dimensions={0} | all-to-all | bytes 524288 | tf_op jit(solution)/shard_map/all_to_all | solution.py:72
  104.1 0.1 reshape.34
  104.2 0.1 all_to_all.14
  104.3 15.9 %all_to_all.20 = f32[16,1,128]{2,1,0:T(1,128)S(1)} all-to-all(f32[16,1,128]{2,1,0:T(1,128)S(1)} %bitcast.30), channel_id=1, replica_groups=mesh['y'=8,'x'=4,'zl'=2,'zh'=4,'c'=2] {'zl','zh','c'}, dimensions={0} | all-to-all | bytes 16384 | tf_op jit(solution)/shard_map/all_to_all | solution.py:74
  120.2 0.7 reshape.35
  (6 shorter events, 0.2 us)
Async XLA Ops:
  0.0 41.7 %copy-start = (f32[2,512,512]{2,1,0:T(8,128)S(1)}, f32[2,512,512]{2,1,0:T(8,128)}, u32[]{:S(2)}) copy-start(f32[2,512,512]{2,1,0:T(8,128)} %param.2) | copy-start | bytes 6291460
  0.0 41.7 %collective-permute-start.2 = (f32[2,512,512]{2,1,0:T(8,128)}, f32[2,512,512]{2,1,0:T(8,128)}, u32[]{:S(2)}, u32[]{:S(2)}) collective-permute-start(f32[2,512,512]{2,1,0:T(8,128)} %param.2), channel_id=1, source_target_pairs={{0,1},{1,0},{2,3},{3,2},{4,5},{5,4},{6,7},{7,6},{8,9},{9,8},{10,11... | collective-permute-start | bytes 6291464 | tf_op jit(solution)/shard_map/ppermute | solution.py:18
  8.9 6.4 %collective-permute-start = (f32[12,512]{1,0:T(8,128)}, f32[12,512]{1,0:T(8,128)S(1)}, u32[]{:S(2)}, u32[]{:S(2)}) collective-permute-start(f32[12,512]{1,0:T(8,128)} %bitcast.31), channel_id=1, source_target_pairs={{32,0},{50,2},{4,4},{22,6},{48,16},{2,18},{20,20},{38,22},{0,32},{... | collective-permute-start | bytes 73736 | tf_op jit(solution)/shard_map/ppermute | solution.py:22
  16.1 18.6 %all-to-all-start = ((f32[32,24,128]{2,1,0:T(8,128)}), f32[32,24,128]{2,1,0:T(8,128)S(1)}, u32[]{:S(2)}, u32[]{:S(2)}) async-start(f32[32,24,128]{2,1,0:T(8,128)} %bitcast.1), calls=%async_computation | async-start | bytes 786432 | tf_op jit(solution)/shard_map/all_to_all | solution.py:27
  35.2 30.3 %collective-permute-start.5 = (f32[96,1024]{1,0:T(8,128)S(1)}, f32[96,1024]{1,0:T(8,128)S(1)}, u32[]{:S(2)}, u32[]{:S(2)}) collective-permute-start(f32[96,1024]{1,0:T(8,128)S(1)} %bitcast.24), channel_id=1, source_target_pairs={{16,0},{49,1},{50,2},{19,3},{20,4},{53,5},{54,6},{23,7},{32,16},{1... | collective-permute-start | bytes 1179656 | tf_op jit(solution)/shard_map/ppermute | solution.py:43
  38.3 16.9 %collective-permute-start.1 = (f32[96,1024]{1,0:T(8,128)S(1)}, f32[96,1024]{1,0:T(8,128)S(1)}, u32[]{:S(2)}, u32[]{:S(2)}) collective-permute-start(f32[96,1024]{1,0:T(8,128)S(1)} %bitcast.25), channel_id=1, source_target_pairs={{48,0},{17,1},{18,2},{51,3},{52,4},{21,5},{22,6},{55,7},{0,16},{33... | collective-permute-start | bytes 1179656 | tf_op jit(solution)/shard_map/ppermute | solution.py:43
  46.0 19.6 %collective-permute-start.6 = (f32[96,1024]{1,0:T(8,128)S(1)}, f32[96,1024]{1,0:T(8,128)S(1)}, u32[]{:S(2)}, u32[]{:S(2)}) collective-permute-start(f32[96,1024]{1,0:T(8,128)S(1)} %fusion.11), channel_id=1, source_target_pairs={{0,2},{1,7},{2,0},{3,5},{4,6},{5,3},{6,4},{7,1},{8,10},{9,15},{10,... | collective-permute-start | bytes 1179656 | tf_op jit(solution)/shard_map/ppermute | solution.py:36
  57.5 11.0 %collective-permute-start.4 = (f32[48,1024]{1,0:T(8,128)S(1)}, f32[48,1024]{1,0:T(8,128)S(1)}, u32[]{:S(2)}, u32[]{:S(2)}) collective-permute-start(f32[48,1024]{1,0:T(8,128)S(1)} %get-tuple-element.12), channel_id=1, source_target_pairs={{0,2},{1,7},{2,0},{3,5},{4,6},{5,3},{6,4},{7,1},{8,10},{9,15},{10,... | collective-permute-start | bytes 589832 | tf_op jit(solution)/shard_map/ppermute | solution.py:36
  62.5 14.4 %collective-permute-start.3 = (f32[96,1024]{1,0:T(8,128)S(1)}, f32[96,1024]{1,0:T(8,128)S(1)}, u32[]{:S(2)}, u32[]{:S(2)}) collective-permute-start(f32[96,1024]{1,0:T(8,128)S(1)} %bitcast.27), channel_id=1, source_target_pairs={{32,0},{48,16},{0,32},{16,48},{33,1},{49,17},{1,33},{17,49},{34,2}... | collective-permute-start | bytes 1179656 | tf_op jit(solution)/shard_map/ppermute | solution.py:58
  68.5 19.3 %collective-permute-start.8 = (f32[96,1024]{1,0:T(8,128)S(1)}, f32[96,1024]{1,0:T(8,128)S(1)}, u32[]{:S(2)}, u32[]{:S(2)}) collective-permute-start(f32[96,1024]{1,0:T(8,128)S(1)} %convolution_add_fusion), channel_id=1, source_target_pairs={{0,6},{1,3},{2,4},{3,1},{4,2},{5,7},{6,0},{7,5},{8,14},{9,11},{10,... | collective-permute-start | bytes 1179656 | tf_op jit(solution)/shard_map/ppermute | solution.py:36
  70.4 17.4 %collective-permute-start.7 = (f32[48,1024]{1,0:T(8,128)S(1)}, f32[48,1024]{1,0:T(8,128)S(1)}, u32[]{:S(2)}, u32[]{:S(2)}) collective-permute-start(f32[48,1024]{1,0:T(8,128)S(1)} %get-tuple-element.11), channel_id=1, source_target_pairs={{0,2},{1,7},{2,0},{3,5},{4,6},{5,3},{6,4},{7,1},{8,10},{9,15},{10,... | collective-permute-start | bytes 589832 | tf_op jit(solution)/shard_map/ppermute | solution.py:36

commit v6 on v5

--- a/solution.py
+++ b/solution.py
@@ -53,7 +53,8 @@
     cut = term_a.shape[0] // 2
     from_a, later_a = paired(term_a[:cut], 0), paired(term_a[cut:], 0)
     near, term_a = lax.optimization_barrier((near, term_a))
-    from_a, sent_b = lax.optimization_barrier((from_a, term(block_b) + passed))
+    term_b = lax.optimization_barrier(term(block_b))
+    from_a, sent_b = lax.optimization_barrier((from_a, term_b + passed))
     from_b = paired(sent_b, 1)
     block = lax.ppermute(near, "x", [((x + 2) % X, x) for x in range(X)])
     mine = lax.optimization_barrier(term(block))

time: 121 us -> 121 us (level)
  no operation moved by 1% of the time
where the time goes in v6:
time: 121 us
  starting transfers between devices  47.9 us (40%)
  blocking collectives  31.2 us (26%)
  waiting for transfers between devices  27.5 us (23%)
  matrix products  9.6 us (8%)
  other arithmetic  2.25 us (2%)
  local copies, waits for them, and re-layouts  2.08 us (2%)
    ppermute x4, starting transfers between devices, paired(): return lax.ppermute(block, ('zh', 'c'), pairs)  22.7 us
    all_to_all x1, blocking collectives, body(): lax.all_to_all(tile.reshape(ZL * ZH * C, m * n), ('zl', 'zh', 'c'), 0, 0,...  15.9 us
    all_to_all x1, blocking collectives, body(): lax.all_to_all(tile.reshape(Y * X, ZL * m, half), ('y', 'x'), 0, 0, tiled...  15.3 us
    all_to_all x1, waiting for transfers between devices, body(): lax.all_to_all(sent.reshape(Y * ZL * C, -1, LANES), ('y', 'zl', 'c'), 0,...  13.8 us
    ppermute x4, waiting for transfers between devices, paired(): return lax.ppermute(block, ('zh', 'c'), pairs)  9.24 us
    ppermute x1, starting transfers between devices, body(): swapped = lax.ppermute(integrals, 'c', [(0, 1), (1, 0)])  8.91 us
    dot_general x4, matrix products, term(): lax.dot_general(block, held, (((1,), (1,)), ((), ())), precision=lax.Prec...  8.77 us
    ppermute x2, starting transfers between devices, fetch(): return lax.ppermute(source, ('x', 'zh', 'c'), pairs)  6.49 us
  transfers between devices with their start and end apart: 10, of which 4 were waited for; matrix products, arithmetic and copies ran while one was open for 10% of the time, Pallas kernels for 0%

profile of v6, /device:TPU:1, one launch (start us, length us, event | category | flops | bytes accessed | tf_op | source)
XLA Modules:
  0.0 120.7 jit_solution(9354565850991646852)
XLA Ops:
  0.0 0.0 copy-start
  0.0 8.9 %collective-permute-start.2 = (f32[2,512,512]{2,1,0:T(8,128)}, f32[2,512,512]{2,1,0:T(8,128)}, u32[]{:S(2)}, u32[]{:S(2)}) collective-permute-start(f32[2,512,512]{2,1,0:T(8,128)} %param.2), channel_id=1, source_target_pairs={{0,1},{1,0},{2,3},{3,2},{4,5},{5,4},{6,7},{7,6},{8,9},{9,8},{10,11... | collective-permute-start | bytes 6291464 | tf_op jit(solution)/shard_map/ppermute | solution.py:18
  8.9 1.9 %collective-permute-start = (f32[12,512]{1,0:T(8,128)}, f32[12,512]{1,0:T(8,128)S(1)}, u32[]{:S(2)}, u32[]{:S(2)}) collective-permute-start(f32[12,512]{1,0:T(8,128)} %bitcast.31), channel_id=1, source_target_pairs={{32,0},{50,2},{4,4},{22,6},{48,16},{2,18},{20,20},{38,22},{0,32},{... | collective-permute-start | bytes 73736 | tf_op jit(solution)/shard_map/ppermute | solution.py:22
  10.8 4.4 %collective-permute-done = f32[12,512]{1,0:T(8,128)S(1)} collective-permute-done((f32[12,512]{1,0:T(8,128)}, f32[12,512]{1,0:T(8,128)S(1)}, u32[]{:S(2)}, u32[]{:S(2)}) %collective-permute-start) | collective-permute-done | bytes 24608 | tf_op jit(solution)/shard_map/ppermute | solution.py:22
  15.3 0.8 broadcast_in_dim.3
  16.1 4.9 %all-to-all-start = ((f32[32,24,128]{2,1,0:T(8,128)}), f32[32,24,128]{2,1,0:T(8,128)S(1)}, u32[]{:S(2)}, u32[]{:S(2)}) async-start(f32[32,24,128]{2,1,0:T(8,128)} %bitcast.1), calls=%async_computation | async-start | bytes 786432 | tf_op jit(solution)/shard_map/all_to_all | solution.py:27
  20.9 13.8 %all-to-all-done = f32[32,24,128]{2,1,0:T(8,128)S(1)} async-done(((f32[32,24,128]{2,1,0:T(8,128)}), f32[32,24,128]{2,1,0:T(8,128)S(1)}, u32[]{:S(2)}, u32[]{:S(2)}) %all-to-all-start) | async-done | bytes 393248 | tf_op jit(solution)/shard_map/all_to_all | solution.py:27
  34.7 0.1 reshape.30
  34.8 0.3 copy.6
  35.1 0.1 copy.9
  35.2 3.1 %collective-permute-start.5 = (f32[96,1024]{1,0:T(8,128)S(1)}, f32[96,1024]{1,0:T(8,128)S(1)}, u32[]{:S(2)}, u32[]{:S(2)}) collective-permute-start(f32[96,1024]{1,0:T(8,128)S(1)} %bitcast.24), channel_id=1, source_target_pairs={{16,0},{49,1},{50,2},{19,3},{20,4},{53,5},{54,6},{23,7},{32,16},{1... | collective-permute-start | bytes 1179656 | tf_op jit(solution)/shard_map/ppermute | solution.py:43
  38.3 3.4 %collective-permute-start.1 = (f32[96,1024]{1,0:T(8,128)S(1)}, f32[96,1024]{1,0:T(8,128)S(1)}, u32[]{:S(2)}, u32[]{:S(2)}) collective-permute-start(f32[96,1024]{1,0:T(8,128)S(1)} %bitcast.25), channel_id=1, source_target_pairs={{48,0},{17,1},{18,2},{51,3},{52,4},{21,5},{22,6},{55,7},{0,16},{33... | collective-permute-start | bytes 1179656 | tf_op jit(solution)/shard_map/ppermute | solution.py:43
  41.7 0.0 collective-permute-done.2
  41.7 0.0 copy-done
  41.7 2.0 %pad_maximum_fusion = f32[2,512,1024]{2,1,0:T(8,128)S(1)} fusion(f32[2,512,512]{2,1,0:T(8,128)} %collective-permute-done.2, f32[2,512,512]{2,1,0:T(8,128)S(1)} %copy-done), kind=kLoop, calls=%fused_computation | loop fusion | flops 1048576 | bytes 8388608 | tf_op jit(solution)/shard_map/concatenate | solution.py:19
  43.8 2.2 %fusion.12 = f32[96,1024]{1,0:T(8,128)S(1)} fusion(f32[96,1024]{1,0:T(8,128)S(1)} %bitcast.26, f32[1024,1024]{1,0:T(8,128)S(1)} %bitcast.20), kind=kOutput, calls=%fused_computation.16 | convolution fusion | flops 603979776 | bytes 4980736 | tf_op jit(solution)/shard_map/dot_general | solution.py:46
  46.0 9.3 %collective-permute-start.6 = (f32[96,1024]{1,0:T(8,128)S(1)}, f32[96,1024]{1,0:T(8,128)S(1)}, u32[]{:S(2)}, u32[]{:S(2)}) collective-permute-start(f32[96,1024]{1,0:T(8,128)S(1)} %fusion.12), channel_id=1, source_target_pairs={{0,2},{1,7},{2,0},{3,5},{4,6},{5,3},{6,4},{7,1},{8,10},{9,15},{10,... | collective-permute-start | bytes 1179656 | tf_op jit(solution)/shard_map/ppermute | solution.py:36
  55.3 0.0 collective-permute-done.1
  55.3 2.2 %fusion.9 = f32[96,1024]{1,0:T(8,128)S(1)} fusion(f32[96,1024]{1,0:T(8,128)S(1)} %collective-permute-done.1, f32[1024,1024]{1,0:T(8,128)S(1)} %bitcast.21), kind=kOutput, calls=%fused_computation.13 | convolution fusion | flops 603979776 | bytes 4980736 | tf_op jit(solution)/shard_map/dot_general | solution.py:46
  57.5 5.0 %collective-permute-start.4 = (f32[48,1024]{1,0:T(8,128)S(1)}, f32[48,1024]{1,0:T(8,128)S(1)}, u32[]{:S(2)}, u32[]{:S(2)}) collective-permute-start(f32[48,1024]{1,0:T(8,128)S(1)} %get-tuple-element.12), channel_id=1, source_target_pairs={{0,2},{1,7},{2,0},{3,5},{4,6},{5,3},{6,4},{7,1},{8,10},{9,15},{10,... | collective-permute-start | bytes 589832 | tf_op jit(solution)/shard_map/ppermute | solution.py:36
  62.5 3.0 %collective-permute-start.3 = (f32[96,1024]{1,0:T(8,128)S(1)}, f32[96,1024]{1,0:T(8,128)S(1)}, u32[]{:S(2)}, u32[]{:S(2)}) collective-permute-start(f32[96,1024]{1,0:T(8,128)S(1)} %bitcast.27), channel_id=1, source_target_pairs={{32,0},{48,16},{0,32},{16,48},{33,1},{49,17},{1,33},{17,49},{34,2}... | collective-permute-start | bytes 1179656 | tf_op jit(solution)/shard_map/ppermute | solution.py:59
  65.5 0.0 collective-permute-done.5
  65.6 2.2 %fusion.11 = f32[96,1024]{1,0:T(8,128)S(1)} fusion(f32[96,1024]{1,0:T(8,128)S(1)} %collective-permute-done.5, f32[1024,1024]{1,0:T(8,128)S(1)} %bitcast.22), kind=kOutput, calls=%fused_computation.15 | convolution fusion | flops 603979776 | bytes 4980736 | tf_op jit(solution)/shard_map/dot_general | solution.py:46
  67.8 0.0 collective-permute-done.6
  67.8 0.7 collective-permute-done.4
  68.5 1.9 %collective-permute-start.8 = (f32[96,1024]{1,0:T(8,128)S(1)}, f32[96,1024]{1,0:T(8,128)S(1)}, u32[]{:S(2)}, u32[]{:S(2)}) collective-permute-start(f32[96,1024]{1,0:T(8,128)S(1)} %add.12), channel_id=1, source_target_pairs={{0,6},{1,3},{2,4},{3,1},{4,2},{5,7},{6,0},{7,5},{8,14},{9,11},{10,... | collective-permute-start | bytes 1179656 | tf_op jit(solution)/shard_map/ppermute | solution.py:36
  70.4 6.5 %collective-permute-start.7 = (f32[48,1024]{1,0:T(8,128)S(1)}, f32[48,1024]{1,0:T(8,128)S(1)}, u32[]{:S(2)}, u32[]{:S(2)}) collective-permute-start(f32[48,1024]{1,0:T(8,128)S(1)} %get-tuple-element.11), channel_id=1, source_target_pairs={{0,2},{1,7},{2,0},{3,5},{4,6},{5,3},{6,4},{7,1},{8,10},{9,15},{10,... | collective-permute-start | bytes 589832 | tf_op jit(solution)/shard_map/ppermute | solution.py:36
  76.9 0.0 collective-permute-done.3
  76.9 2.2 %fusion.10 = f32[96,1024]{1,0:T(8,128)S(1)} fusion(f32[96,1024]{1,0:T(8,128)S(1)} %collective-permute-done.3, f32[1024,1024]{1,0:T(8,128)S(1)} %bitcast.23), kind=kOutput, calls=%fused_computation.14 | convolution fusion | flops 603979776 | bytes 4980736 | tf_op jit(solution)/shard_map/dot_general | solution.py:46
  79.1 8.6 %collective-permute-done.7 = f32[48,1024]{1,0:T(8,128)S(1)} collective-permute-done((f32[48,1024]{1,0:T(8,128)S(1)}, f32[48,1024]{1,0:T(8,128)S(1)}, u32[]{:S(2)}, u32[]{:S(2)}) %collective-permute-start.7) | collective-permute-done | bytes 196640 | tf_op jit(solution)/shard_map/ppermute | solution.py:36
  87.7 0.0 collective-permute-done.8
  87.7 0.1 fusion.2
  87.8 0.4 fusion.3
  88.2 0.4 fusion
  88.6 15.3 %all_to_all.19 = f32[32,8,256]{2,1,0:T(8,128)S(1)} all-to-all(f32[32,8,256]{2,1,0:T(8,128)S(1)} %fusion), channel_id=1, replica_groups=mesh['y'=8,'x'=4,'zl'=2,'zh'=4,'c'=2] {'y','x'}, dimensions={0} | all-to-all | bytes 524288 | tf_op jit(solution)/shard_map/all_to_all | solution.py:73
  104.0 0.1 reshape.34
  104.1 0.1 all_to_all.14
  104.2 15.9 %all_to_all.20 = f32[16,1,128]{2,1,0:T(1,128)S(1)} all-to-all(f32[16,1,128]{2,1,0:T(1,128)S(1)} %bitcast.30), channel_id=1, replica_groups=mesh['y'=8,'x'=4,'zl'=2,'zh'=4,'c'=2] {'zl','zh','c'}, dimensions={0} | all-to-all | bytes 16384 | tf_op jit(solution)/shard_map/all_to_all | solution.py:75
  120.1 0.7 reshape.35
  (7 shorter events, 0.2 us)
Async XLA Ops:
  0.0 41.7 %copy-start = (f32[2,512,512]{2,1,0:T(8,128)S(1)}, f32[2,512,512]{2,1,0:T(8,128)}, u32[]{:S(2)}) copy-start(f32[2,512,512]{2,1,0:T(8,128)} %param.2) | copy-start | bytes 6291460
  0.0 41.7 %collective-permute-start.2 = (f32[2,512,512]{2,1,0:T(8,128)}, f32[2,512,512]{2,1,0:T(8,128)}, u32[]{:S(2)}, u32[]{:S(2)}) collective-permute-start(f32[2,512,512]{2,1,0:T(8,128)} %param.2), channel_id=1, source_target_pairs={{0,1},{1,0},{2,3},{3,2},{4,5},{5,4},{6,7},{7,6},{8,9},{9,8},{10,11... | collective-permute-start | bytes 6291464 | tf_op jit(solution)/shard_map/ppermute | solution.py:18
  8.9 6.4 %collective-permute-start = (f32[12,512]{1,0:T(8,128)}, f32[12,512]{1,0:T(8,128)S(1)}, u32[]{:S(2)}, u32[]{:S(2)}) collective-permute-start(f32[12,512]{1,0:T(8,128)} %bitcast.31), channel_id=1, source_target_pairs={{32,0},{50,2},{4,4},{22,6},{48,16},{2,18},{20,20},{38,22},{0,32},{... | collective-permute-start | bytes 73736 | tf_op jit(solution)/shard_map/ppermute | solution.py:22
  16.1 18.6 %all-to-all-start = ((f32[32,24,128]{2,1,0:T(8,128)}), f32[32,24,128]{2,1,0:T(8,128)S(1)}, u32[]{:S(2)}, u32[]{:S(2)}) async-start(f32[32,24,128]{2,1,0:T(8,128)} %bitcast.1), calls=%async_computation | async-start | bytes 786432 | tf_op jit(solution)/shard_map/all_to_all | solution.py:27
  35.2 30.3 %collective-permute-start.5 = (f32[96,1024]{1,0:T(8,128)S(1)}, f32[96,1024]{1,0:T(8,128)S(1)}, u32[]{:S(2)}, u32[]{:S(2)}) collective-permute-start(f32[96,1024]{1,0:T(8,128)S(1)} %bitcast.24), channel_id=1, source_target_pairs={{16,0},{49,1},{50,2},{19,3},{20,4},{53,5},{54,6},{23,7},{32,16},{1... | collective-permute-start | bytes 1179656 | tf_op jit(solution)/shard_map/ppermute | solution.py:43
  38.3 16.9 %collective-permute-start.1 = (f32[96,1024]{1,0:T(8,128)S(1)}, f32[96,1024]{1,0:T(8,128)S(1)}, u32[]{:S(2)}, u32[]{:S(2)}) collective-permute-start(f32[96,1024]{1,0:T(8,128)S(1)} %bitcast.25), channel_id=1, source_target_pairs={{48,0},{17,1},{18,2},{51,3},{52,4},{21,5},{22,6},{55,7},{0,16},{33... | collective-permute-start | bytes 1179656 | tf_op jit(solution)/shard_map/ppermute | solution.py:43
  46.0 21.8 %collective-permute-start.6 = (f32[96,1024]{1,0:T(8,128)S(1)}, f32[96,1024]{1,0:T(8,128)S(1)}, u32[]{:S(2)}, u32[]{:S(2)}) collective-permute-start(f32[96,1024]{1,0:T(8,128)S(1)} %fusion.12), channel_id=1, source_target_pairs={{0,2},{1,7},{2,0},{3,5},{4,6},{5,3},{6,4},{7,1},{8,10},{9,15},{10,... | collective-permute-start | bytes 1179656 | tf_op jit(solution)/shard_map/ppermute | solution.py:36
  57.5 11.0 %collective-permute-start.4 = (f32[48,1024]{1,0:T(8,128)S(1)}, f32[48,1024]{1,0:T(8,128)S(1)}, u32[]{:S(2)}, u32[]{:S(2)}) collective-permute-start(f32[48,1024]{1,0:T(8,128)S(1)} %get-tuple-element.12), channel_id=1, source_target_pairs={{0,2},{1,7},{2,0},{3,5},{4,6},{5,3},{6,4},{7,1},{8,10},{9,15},{10,... | collective-permute-start | bytes 589832 | tf_op jit(solution)/shard_map/ppermute | solution.py:36
  62.5 14.4 %collective-permute-start.3 = (f32[96,1024]{1,0:T(8,128)S(1)}, f32[96,1024]{1,0:T(8,128)S(1)}, u32[]{:S(2)}, u32[]{:S(2)}) collective-permute-start(f32[96,1024]{1,0:T(8,128)S(1)} %bitcast.27), channel_id=1, source_target_pairs={{32,0},{48,16},{0,32},{16,48},{33,1},{49,17},{1,33},{17,49},{34,2}... | collective-permute-start | bytes 1179656 | tf_op jit(solution)/shard_map/ppermute | solution.py:59
  68.5 19.2 %collective-permute-start.8 = (f32[96,1024]{1,0:T(8,128)S(1)}, f32[96,1024]{1,0:T(8,128)S(1)}, u32[]{:S(2)}, u32[]{:S(2)}) collective-permute-start(f32[96,1024]{1,0:T(8,128)S(1)} %add.12), channel_id=1, source_target_pairs={{0,6},{1,3},{2,4},{3,1},{4,2},{5,7},{6,0},{7,5},{8,14},{9,11},{10,... | collective-permute-start | bytes 1179656 | tf_op jit(solution)/shard_map/ppermute | solution.py:36
  70.4 17.3 %collective-permute-start.7 = (f32[48,1024]{1,0:T(8,128)S(1)}, f32[48,1024]{1,0:T(8,128)S(1)}, u32[]{:S(2)}, u32[]{:S(2)}) collective-permute-start(f32[48,1024]{1,0:T(8,128)S(1)} %get-tuple-element.11), channel_id=1, source_target_pairs={{0,2},{1,7},{2,0},{3,5},{4,6},{5,3},{6,4},{7,1},{8,10},{9,15},{10,... | collective-permute-start | bytes 589832 | tf_op jit(solution)/shard_map/ppermute | solution.py:36

commit v7 on v4

--- a/solution.py
+++ b/solution.py
@@ -15,11 +15,10 @@
     own = occupied.shape[1]
     half = rows // 2
     share = own // C
+    pairs = [((x + d + 2) % X * ZH + d, x * ZH + d) for x in range(X) for d in range(ZH)]
+    moved = lax.ppermute(occupied.T, ("x", "zh"), pairs)
     swapped = lax.ppermute(integrals, "c", [(0, 1), (1, 0)])
     held = jnp.concatenate([integrals, swapped], axis=2).reshape(parts * rows, C * depth)
-
-    pairs = [((x + d + 2) % X * ZH + d, x * ZH + d) for x in range(X) for d in range(ZH)]
-    moved = lax.ppermute(occupied.T, ("x", "zh"), pairs)
     sent = jnp.broadcast_to(
         moved.reshape(C, share * depth // LANES, LANES),
         (Y, ZL, C, share * depth // LANES, LANES),

time: 121 us -> 121 us (level)
  no operation moved by 1% of the time
where the time goes in v7:
time: 121 us; the launch traced here: 120 us
  starting transfers between devices  41.4 us (34%)
  waiting for transfers between devices  32.5 us (27%)
  blocking collectives  32.3 us (27%)
  matrix products  9.61 us (8%)
  other arithmetic  2.21 us (2%)
  local copies, waits for them, and re-layouts  2.04 us (2%)
    all_to_all x1, blocking collectives, body(): lax.all_to_all(tile.reshape(ZL * ZH * C, m * n), ('zl', 'zh', 'c'), 0, 0,...  16.4 us
    ppermute x3, starting transfers between devices, paired(): return lax.ppermute(block, ('zh', 'c'), pairs)  16.2 us
    all_to_all x1, blocking collectives, body(): lax.all_to_all(tile.reshape(Y * X, ZL * m, half), ('y', 'x'), 0, 0, tiled...  15.9 us
    ppermute x3, waiting for transfers between devices, paired(): return lax.ppermute(block, ('zh', 'c'), pairs)  14.3 us
    all_to_all x1, waiting for transfers between devices, body(): lax.all_to_all(sent.reshape(Y * ZL * C, -1, LANES), ('y', 'zl', 'c'), 0,...  13.8 us
    ppermute x1, starting transfers between devices, body(): swapped = lax.ppermute(integrals, 'c', [(0, 1), (1, 0)])  8.91 us
    dot_general x4, matrix products, term(): lax.dot_general(block, held, (((1,), (1,)), ((), ())), precision=lax.Prec...  8.78 us
    ppermute x2, starting transfers between devices, fetch(): return lax.ppermute(source, ('x', 'zh', 'c'), pairs)  6.49 us
  transfers between devices with their start and end apart: 9, of which 4 were waited for; matrix products, arithmetic and copies ran while one was open for 10% of the time, Pallas kernels for 0%

profile of v7, /device:TPU:1, one launch (start us, length us, event | category | flops | bytes accessed | tf_op | source)
XLA Modules:
  0.0 120.2 jit_solution(1867387240211976461)
XLA Ops:
  0.0 0.0 copy-start
  0.0 8.9 %collective-permute-start.2 = (f32[2,512,512]{2,1,0:T(8,128)}, f32[2,512,512]{2,1,0:T(8,128)}, u32[]{:S(2)}, u32[]{:S(2)}) collective-permute-start(f32[2,512,512]{2,1,0:T(8,128)} %param.2), channel_id=1, source_target_pairs={{0,1},{1,0},{2,3},{3,2},{4,5},{5,4},{6,7},{7,6},{8,9},{9,8},{10,11... | collective-permute-start | bytes 6291464 | tf_op jit(solution)/shard_map/ppermute | solution.py:20
  8.9 1.9 %collective-permute-start = (f32[12,512]{1,0:T(8,128)}, f32[12,512]{1,0:T(8,128)S(1)}, u32[]{:S(2)}, u32[]{:S(2)}) collective-permute-start(f32[12,512]{1,0:T(8,128)} %bitcast.31), channel_id=1, source_target_pairs={{32,0},{50,2},{4,4},{22,6},{48,16},{2,18},{20,20},{38,22},{0,32},{... | collective-permute-start | bytes 73736 | tf_op jit(solution)/shard_map/ppermute | solution.py:19
  10.8 4.4 %collective-permute-done = f32[12,512]{1,0:T(8,128)S(1)} collective-permute-done((f32[12,512]{1,0:T(8,128)}, f32[12,512]{1,0:T(8,128)S(1)}, u32[]{:S(2)}, u32[]{:S(2)}) %collective-permute-start) | collective-permute-done | bytes 24608 | tf_op jit(solution)/shard_map/ppermute | solution.py:19
  15.3 0.8 broadcast_in_dim.3
  16.1 4.9 %all-to-all-start = ((f32[32,24,128]{2,1,0:T(8,128)}), f32[32,24,128]{2,1,0:T(8,128)S(1)}, u32[]{:S(2)}, u32[]{:S(2)}) async-start(f32[32,24,128]{2,1,0:T(8,128)} %bitcast.1), calls=%async_computation | async-start | bytes 786432 | tf_op jit(solution)/shard_map/all_to_all | solution.py:26
  20.9 13.8 %all-to-all-done = f32[32,24,128]{2,1,0:T(8,128)S(1)} async-done(((f32[32,24,128]{2,1,0:T(8,128)}), f32[32,24,128]{2,1,0:T(8,128)S(1)}, u32[]{:S(2)}, u32[]{:S(2)}) %all-to-all-start) | async-done | bytes 393248 | tf_op jit(solution)/shard_map/all_to_all | solution.py:26
  34.7 0.1 reshape.30
  34.8 0.3 copy.6
  35.1 0.1 copy.9
  35.2 3.1 %collective-permute-start.5 = (f32[96,1024]{1,0:T(8,128)S(1)}, f32[96,1024]{1,0:T(8,128)S(1)}, u32[]{:S(2)}, u32[]{:S(2)}) collective-permute-start(f32[96,1024]{1,0:T(8,128)S(1)} %bitcast.24), channel_id=1, source_target_pairs={{16,0},{49,1},{50,2},{19,3},{20,4},{53,5},{54,6},{23,7},{32,16},{1... | collective-permute-start | bytes 1179656 | tf_op jit(solution)/shard_map/ppermute | solution.py:42
  38.3 3.4 %collective-permute-start.1 = (f32[96,1024]{1,0:T(8,128)S(1)}, f32[96,1024]{1,0:T(8,128)S(1)}, u32[]{:S(2)}, u32[]{:S(2)}) collective-permute-start(f32[96,1024]{1,0:T(8,128)S(1)} %bitcast.25), channel_id=1, source_target_pairs={{48,0},{17,1},{18,2},{51,3},{52,4},{21,5},{22,6},{55,7},{0,16},{33... | collective-permute-start | bytes 1179656 | tf_op jit(solution)/shard_map/ppermute | solution.py:42
  41.7 0.0 collective-permute-done.2
  41.7 0.0 copy-done
  41.7 2.0 %pad_maximum_fusion = f32[2,512,1024]{2,1,0:T(8,128)S(1)} fusion(f32[2,512,512]{2,1,0:T(8,128)} %collective-permute-done.2, f32[2,512,512]{2,1,0:T(8,128)S(1)} %copy-done), kind=kLoop, calls=%fused_computation | loop fusion | flops 1048576 | bytes 8388608 | tf_op jit(solution)/shard_map/concatenate | solution.py:21
  43.8 2.2 %fusion.9 = f32[96,1024]{1,0:T(8,128)S(1)} fusion(f32[96,1024]{1,0:T(8,128)S(1)} %bitcast.26, f32[1024,1024]{1,0:T(8,128)S(1)} %bitcast.20), kind=kOutput, calls=%fused_computation.14 | convolution fusion | flops 603979776 | bytes 4980736 | tf_op jit(solution)/shard_map/dot_general | solution.py:45
  46.0 9.3 %collective-permute-start.6 = (f32[96,1024]{1,0:T(8,128)S(1)}, f32[96,1024]{1,0:T(8,128)S(1)}, u32[]{:S(2)}, u32[]{:S(2)}) collective-permute-start(f32[96,1024]{1,0:T(8,128)S(1)} %fusion.9), channel_id=1, source_target_pairs={{0,2},{1,7},{2,0},{3,5},{4,6},{5,3},{6,4},{7,1},{8,10},{9,15},{10,... | collective-permute-start | bytes 1179656 | tf_op jit(solution)/shard_map/ppermute | solution.py:35
  55.3 0.0 collective-permute-done.1
  55.3 2.2 %fusion.7 = f32[96,1024]{1,0:T(8,128)S(1)} fusion(f32[96,1024]{1,0:T(8,128)S(1)} %collective-permute-done.1, f32[1024,1024]{1,0:T(8,128)S(1)} %bitcast.21), kind=kOutput, calls=%fused_computation.12 | convolution fusion | flops 603979776 | bytes 4980736 | tf_op jit(solution)/shard_map/dot_general | solution.py:45
  57.5 5.0 %collective-permute-start.4 = (f32[96,1024]{1,0:T(8,128)S(1)}, f32[96,1024]{1,0:T(8,128)S(1)}, u32[]{:S(2)}, u32[]{:S(2)}) collective-permute-start(f32[96,1024]{1,0:T(8,128)S(1)} %fusion.7), channel_id=1, source_target_pairs={{0,2},{1,7},{2,0},{3,5},{4,6},{5,3},{6,4},{7,1},{8,10},{9,15},{10,... | collective-permute-start | bytes 1179656 | tf_op jit(solution)/shard_map/ppermute | solution.py:35
  62.5 3.0 %collective-permute-start.3 = (f32[96,1024]{1,0:T(8,128)S(1)}, f32[96,1024]{1,0:T(8,128)S(1)}, u32[]{:S(2)}, u32[]{:S(2)}) collective-permute-start(f32[96,1024]{1,0:T(8,128)S(1)} %bitcast.27), channel_id=1, source_target_pairs={{32,0},{48,16},{0,32},{16,48},{33,1},{49,17},{1,33},{17,49},{34,2}... | collective-permute-start | bytes 1179656 | tf_op jit(solution)/shard_map/ppermute | solution.py:56
  65.5 0.0 collective-permute-done.5
  65.5 0.0 collective-permute-done.6
  65.5 2.2 %convolution_add_fusion = f32[96,1024]{1,0:T(8,128)S(1)} fusion(f32[96,1024]{1,0:T(8,128)S(1)} %collective-permute-done.6, f32[96,1024]{1,0:T(8,128)S(1)} %collective-permute-done.5, f32[1024,1024]{1,0:T(8,128)S(1)} %bitcast.22), kind=kOutput, calls=%fused_computation.1 | convolution fusion | flops 604078080 | bytes 5373952 | tf_op jit(solution)/shard_map/dot_general | solution.py:45
  67.7 4.7 %collective-permute-done.4 = f32[96,1024]{1,0:T(8,128)S(1)} collective-permute-done((f32[96,1024]{1,0:T(8,128)S(1)}, f32[96,1024]{1,0:T(8,128)S(1)}, u32[]{:S(2)}, u32[]{:S(2)}) %collective-permute-start.4) | collective-permute-done | bytes 393248 | tf_op jit(solution)/shard_map/ppermute | solution.py:35
  72.4 1.9 %collective-permute-start.7 = (f32[96,1024]{1,0:T(8,128)S(1)}, f32[96,1024]{1,0:T(8,128)S(1)}, u32[]{:S(2)}, u32[]{:S(2)}) collective-permute-start(f32[96,1024]{1,0:T(8,128)S(1)} %convolution_add_fusion), channel_id=1, source_target_pairs={{0,6},{1,3},{2,4},{3,1},{4,2},{5,7},{6,0},{7,5},{8,14},{9,11},{10,... | collective-permute-start | bytes 1179656 | tf_op jit(solution)/shard_map/ppermute | solution.py:35
  74.3 0.0 collective-permute-done.3
  74.3 2.2 %fusion.8 = f32[96,1024]{1,0:T(8,128)S(1)} fusion(f32[96,1024]{1,0:T(8,128)S(1)} %collective-permute-done.3, f32[1024,1024]{1,0:T(8,128)S(1)} %bitcast.23), kind=kOutput, calls=%fused_computation.13 | convolution fusion | flops 603979776 | bytes 4980736 | tf_op jit(solution)/shard_map/dot_general | solution.py:45
  76.5 9.6 %collective-permute-done.7 = f32[96,1024]{1,0:T(8,128)S(1)} collective-permute-done((f32[96,1024]{1,0:T(8,128)S(1)}, f32[96,1024]{1,0:T(8,128)S(1)}, u32[]{:S(2)}, u32[]{:S(2)}) %collective-permute-start.7) | collective-permute-done | bytes 393248 | tf_op jit(solution)/shard_map/ppermute | solution.py:35
  86.1 0.1 add_add_fusion
  86.2 0.4 fusion.2
  86.6 0.4 fusion
  87.0 15.9 %all_to_all.19 = f32[32,8,256]{2,1,0:T(8,128)S(1)} all-to-all(f32[32,8,256]{2,1,0:T(8,128)S(1)} %fusion), channel_id=1, replica_groups=mesh['y'=8,'x'=4,'zl'=2,'zh'=4,'c'=2] {'y','x'}, dimensions={0} | all-to-all | bytes 524288 | tf_op jit(solution)/shard_map/all_to_all | solution.py:70
  102.9 0.1 reshape.34
  103.0 0.1 all_to_all.14
  103.1 16.4 %all_to_all.20 = f32[16,1,128]{2,1,0:T(1,128)S(1)} all-to-all(f32[16,1,128]{2,1,0:T(1,128)S(1)} %bitcast.30), channel_id=1, replica_groups=mesh['y'=8,'x'=4,'zl'=2,'zh'=4,'c'=2] {'zl','zh','c'}, dimensions={0} | all-to-all | bytes 16384 | tf_op jit(solution)/shard_map/all_to_all | solution.py:72
  119.6 0.7 reshape.35
  (5 shorter events, 0.1 us)
Async XLA Ops:
  0.0 41.7 %copy-start = (f32[2,512,512]{2,1,0:T(8,128)S(1)}, f32[2,512,512]{2,1,0:T(8,128)}, u32[]{:S(2)}) copy-start(f32[2,512,512]{2,1,0:T(8,128)} %param.2) | copy-start | bytes 6291460
  0.0 41.7 %collective-permute-start.2 = (f32[2,512,512]{2,1,0:T(8,128)}, f32[2,512,512]{2,1,0:T(8,128)}, u32[]{:S(2)}, u32[]{:S(2)}) collective-permute-start(f32[2,512,512]{2,1,0:T(8,128)} %param.2), channel_id=1, source_target_pairs={{0,1},{1,0},{2,3},{3,2},{4,5},{5,4},{6,7},{7,6},{8,9},{9,8},{10,11... | collective-permute-start | bytes 6291464 | tf_op jit(solution)/shard_map/ppermute | solution.py:20
  8.9 6.4 %collective-permute-start = (f32[12,512]{1,0:T(8,128)}, f32[12,512]{1,0:T(8,128)S(1)}, u32[]{:S(2)}, u32[]{:S(2)}) collective-permute-start(f32[12,512]{1,0:T(8,128)} %bitcast.31), channel_id=1, source_target_pairs={{32,0},{50,2},{4,4},{22,6},{48,16},{2,18},{20,20},{38,22},{0,32},{... | collective-permute-start | bytes 73736 | tf_op jit(solution)/shard_map/ppermute | solution.py:19
  16.1 18.6 %all-to-all-start = ((f32[32,24,128]{2,1,0:T(8,128)}), f32[32,24,128]{2,1,0:T(8,128)S(1)}, u32[]{:S(2)}, u32[]{:S(2)}) async-start(f32[32,24,128]{2,1,0:T(8,128)} %bitcast.1), calls=%async_computation | async-start | bytes 786432 | tf_op jit(solution)/shard_map/all_to_all | solution.py:26
  35.2 30.3 %collective-permute-start.5 = (f32[96,1024]{1,0:T(8,128)S(1)}, f32[96,1024]{1,0:T(8,128)S(1)}, u32[]{:S(2)}, u32[]{:S(2)}) collective-permute-start(f32[96,1024]{1,0:T(8,128)S(1)} %bitcast.24), channel_id=1, source_target_pairs={{16,0},{49,1},{50,2},{19,3},{20,4},{53,5},{54,6},{23,7},{32,16},{1... | collective-permute-start | bytes 1179656 | tf_op jit(solution)/shard_map/ppermute | solution.py:42
  38.3 16.9 %collective-permute-start.1 = (f32[96,1024]{1,0:T(8,128)S(1)}, f32[96,1024]{1,0:T(8,128)S(1)}, u32[]{:S(2)}, u32[]{:S(2)}) collective-permute-start(f32[96,1024]{1,0:T(8,128)S(1)} %bitcast.25), channel_id=1, source_target_pairs={{48,0},{17,1},{18,2},{51,3},{52,4},{21,5},{22,6},{55,7},{0,16},{33... | collective-permute-start | bytes 1179656 | tf_op jit(solution)/shard_map/ppermute | solution.py:42
  46.0 19.5 %collective-permute-start.6 = (f32[96,1024]{1,0:T(8,128)S(1)}, f32[96,1024]{1,0:T(8,128)S(1)}, u32[]{:S(2)}, u32[]{:S(2)}) collective-permute-start(f32[96,1024]{1,0:T(8,128)S(1)} %fusion.9), channel_id=1, source_target_pairs={{0,2},{1,7},{2,0},{3,5},{4,6},{5,3},{6,4},{7,1},{8,10},{9,15},{10,... | collective-permute-start | bytes 1179656 | tf_op jit(solution)/shard_map/ppermute | solution.py:35
  57.5 14.9 %collective-permute-start.4 = (f32[96,1024]{1,0:T(8,128)S(1)}, f32[96,1024]{1,0:T(8,128)S(1)}, u32[]{:S(2)}, u32[]{:S(2)}) collective-permute-start(f32[96,1024]{1,0:T(8,128)S(1)} %fusion.7), channel_id=1, source_target_pairs={{0,2},{1,7},{2,0},{3,5},{4,6},{5,3},{6,4},{7,1},{8,10},{9,15},{10,... | collective-permute-start | bytes 1179656 | tf_op jit(solution)/shard_map/ppermute | solution.py:35
  62.5 11.8 %collective-permute-start.3 = (f32[96,1024]{1,0:T(8,128)S(1)}, f32[96,1024]{1,0:T(8,128)S(1)}, u32[]{:S(2)}, u32[]{:S(2)}) collective-permute-start(f32[96,1024]{1,0:T(8,128)S(1)} %bitcast.27), channel_id=1, source_target_pairs={{32,0},{48,16},{0,32},{16,48},{33,1},{49,17},{1,33},{17,49},{34,2}... | collective-permute-start | bytes 1179656 | tf_op jit(solution)/shard_map/ppermute | solution.py:56
  72.4 13.7 %collective-permute-start.7 = (f32[96,1024]{1,0:T(8,128)S(1)}, f32[96,1024]{1,0:T(8,128)S(1)}, u32[]{:S(2)}, u32[]{:S(2)}) collective-permute-start(f32[96,1024]{1,0:T(8,128)S(1)} %convolution_add_fusion), channel_id=1, source_target_pairs={{0,6},{1,3},{2,4},{3,1},{4,2},{5,7},{6,0},{7,5},{8,14},{9,11},{10,... | collective-permute-start | bytes 1179656 | tf_op jit(solution)/shard_map/ppermute | solution.py:35
